TPU v7x, 32 devices: a whole 2x2x4 slice. The times are simulated.
32 devices in a mesh: expert: 8 (over z, y), shard: 4 (over x, core).
Axes of the slice: x: 2, y: 2, z: 4, core: 2. Of those that a mesh axis runs over, the one named last changes fastest.
Arguments:
- inputs: bfloat16 [8192, 768], P('expert'), may hold values from -6 to 6
- cotangent: bfloat16 [8192, 768], P('expert'), may hold values from -6 to 6
- expert_id: int32 [8192], P('expert'), may hold values from 0 to 7, as said below
- slot_index: int32 [8192], P('expert'), may hold values from 0 to 256, as said below
- bucket_ids: int32 [1024, 1024], replicated, may hold values from 0 to 31, as said below
- attention_gain: float32 [768], replicated, may hold values from 0.5 to 1.5
- query_weight: bfloat16 [768, 768], P(None, 'shard'), may hold values from -0.21875 to 0.21875
- key_weight: bfloat16 [768, 768], P(None, 'shard'), may hold values from -0.21875 to 0.21875
- value_weight: bfloat16 [768, 768], P(None, 'shard'), may hold values from -0.21875 to 0.21875
- output_weight: bfloat16 [768, 768], P('shard'), may hold values from -3.5 to 3.5
- bias_table: float32 [32, 12], P(None, 'shard'), may hold values from -5 to 5
- expert_gain: float32 [768], replicated, may hold values from 0.5 to 1.5
- router_weight: bfloat16 [768, 8], replicated, may hold values from -0.109375 to 0.109375
- expert_in: bfloat16 [8, 768, 3072], P('expert', None, 'shard'), may hold values from -0.21875 to 0.21875
- expert_out: bfloat16 [8, 3072, 768], P('expert', 'shard'), may hold values from -12 to 12
Outputs:
- result: bfloat16 [8192, 768], P('expert')
- input_gradient: float32 [8192, 768], P('expert')
- attention_gain_gradient: float32 [768], replicated
- query_gradient: float32 [768, 768], P(None, 'shard')
- key_gradient: float32 [768, 768], P(None, 'shard')
- value_gradient: float32 [768, 768], P(None, 'shard')
- output_weight_gradient: float32 [768, 768], P('shard')
- bias_table_gradient: float32 [32, 12], P(None, 'shard')
- expert_gain_gradient: float32 [768], replicated
- router_gradient: float32 [768, 8], replicated
- expert_in_gradient: float32 [8, 768, 3072], P('expert', None, 'shard')
- expert_out_gradient: float32 [8, 3072, 768], P('expert', 'shard')
Inputs may be any that keep to these rules, and one draw needn't show every extreme that they name: `expert_id`: in every sequence exactly 257 tokens go to one expert, the same one for all sequences; every other expert receives fewer tokens of a sequence than that. slot_index is the rank of the token, in some order, among the tokens of its sequence that go to the same expert; tokens whose slot_index is 192 or more are dropped. bucket_ids[a, c] depends only on c - a.
All inputs are finite; a program needn't handle non-finite values.
Results may differ from a plain program's by a relative error of at most 0.018.
Values may be sent and summed in bfloat16 or wider, within the bound.
No kernel may reach another device: no remote copies, remote signals or barrier semaphores. Data moves between devices by JAX's collectives and lax.ppermute only.
A program may use at most 192 MiB of HBM per device.

v0:
```python
import jax
import jax.numpy as jnp
from jax import lax
from jax.sharding import PartitionSpec as P


def rms_norm(values, gain_values):
    return (
        values * lax.rsqrt(jnp.mean(values * values, axis=-1, keepdims=True) + 1e-06) * gain_values
    )


def table_split(table):
    upper = lax.optimization_barrier(table.astype(jnp.bfloat16))
    remain = table - upper.astype(jnp.float32)
    middle = lax.optimization_barrier(remain.astype(jnp.bfloat16))
    lowest = (remain - middle.astype(jnp.float32)).astype(jnp.bfloat16)
    return jnp.concatenate([upper, middle, lowest], axis=1)


def on_device(
    inputs,
    cotangent,
    expert_id,
    slot_index,
    bucket_ids,
    attention_gain,
    query_weight,
    key_weight,
    value_weight,
    output_weight,
    bias_table,
    expert_gain,
    router_weight,
    expert_in,
    expert_out,
):
    length, model_width = inputs.shape
    heads_here = bias_table.shape[1]
    buckets = bias_table.shape[0]
    head_size = query_weight.shape[1] // heads_here
    experts = router_weight.shape[1]
    local_count = expert_in.shape[0]
    expert_devices = lax.axis_size("expert")
    shard_devices = lax.axis_size("shard")
    capacity = shard_devices * max(1, 3 * length // (2 * experts * shard_devices))
    block_rows = min(512, length)
    block_count = length // block_rows
    target = jnp.where(slot_index < capacity, expert_id * capacity + slot_index, experts * capacity)
    inverse = jnp.full((experts * capacity + 1,), length, jnp.int32)
    inverse = (
        inverse.at[target].set(jnp.arange(length, dtype=jnp.int32))[:-1].reshape(experts, capacity)
    )
    picked = inverse
    zero_row = jnp.zeros((1, model_width), jnp.bfloat16)

    def pack(source_rows):
        return jnp.concatenate([source_rows, zero_row], axis=0)[picked]

    def unpack(arrived):
        flat_rows = arrived.reshape(experts * capacity, model_width)
        return jnp.concatenate([flat_rows, zero_row], axis=0)[target]

    def to_owner(buffer):
        arrived = lax.all_to_all(buffer, "expert", split_axis=0, concat_axis=0, tiled=True)
        return arrived.reshape(expert_devices, local_count, capacity, model_width)

    def to_home(partial_sums):
        merged = partial_sums.reshape(expert_devices * local_count, capacity, model_width)
        summed = lax.psum(merged, "shard")
        arrived = lax.all_to_all(
            summed.astype(jnp.bfloat16), "expert", split_axis=0, concat_axis=0, tiled=True
        )
        return arrived

    def over_heads(partial_sums):
        return lax.psum(partial_sums, "shard")

    source = inputs.astype(jnp.float32)
    normed_full, first_pull = jax.vjp(rms_norm, source, attention_gain)
    normed = normed_full.astype(jnp.bfloat16)
    queries = jnp.dot(normed, query_weight, preferred_element_type=jnp.float32).astype(jnp.bfloat16)
    keys_all = jnp.dot(normed, key_weight, preferred_element_type=jnp.float32).astype(jnp.bfloat16)
    values_all = jnp.dot(normed, value_weight, preferred_element_type=jnp.float32).astype(
        jnp.bfloat16
    )
    query_heads = queries.reshape(length, heads_here, head_size)
    key_heads = keys_all.reshape(length, heads_here, head_size)
    value_heads = values_all.reshape(length, heads_here, head_size)
    split_table = table_split(bias_table)
    bucket_range = jnp.arange(buckets, dtype=jnp.int32)

    def scores_at(first_row):
        query_block = lax.dynamic_slice_in_dim(query_heads, first_row, block_rows, 0)
        bucket_block = lax.dynamic_slice_in_dim(bucket_ids, first_row, block_rows, 0)
        indicator = (bucket_block[:, :, None] == bucket_range[None, None, :]).astype(jnp.bfloat16)
        bias_block = jnp.einsum(
            "rkb,bc->crk", indicator, split_table, preferred_element_type=jnp.float32
        )
        bias_block = bias_block.reshape(3, heads_here, block_rows, length).sum(axis=0)
        scores = jnp.einsum(
            "rhd,khd->hrk", query_block, key_heads, preferred_element_type=jnp.float32
        )
        return (scores * 0.125 + bias_block, indicator, query_block)

    def forward_block(first_row):
        scores, indicator, query_block = scores_at(first_row)
        row_peak = jnp.max(scores, axis=-1, keepdims=True)
        powered = jnp.exp(scores - row_peak)
        row_total = jnp.sum(powered, axis=-1, keepdims=True)
        weights = (powered / row_total).astype(jnp.bfloat16)
        mixed_block = jnp.einsum(
            "hrk,khd->rhd", weights, value_heads, preferred_element_type=jnp.float32
        )
        return (mixed_block.astype(jnp.bfloat16), (row_peak + jnp.log(row_total))[:, :, 0])

    starts = jnp.arange(block_count, dtype=jnp.int32) * block_rows
    mixed_blocks, log_totals = lax.map(forward_block, starts)
    mixed = mixed_blocks.reshape(length, heads_here * head_size)
    attention = over_heads(jnp.dot(mixed, output_weight, preferred_element_type=jnp.float32))
    middle = source + attention
    routed_full, second_pull = jax.vjp(rms_norm, middle, expert_gain)
    routed = routed_full.astype(jnp.bfloat16)
    logits = jnp.dot(routed, router_weight, preferred_element_type=jnp.float32)
    probability = jax.nn.softmax(logits, axis=-1)
    chosen_mask = (expert_id[:, None] == jnp.arange(experts, dtype=jnp.int32)[None, :]).astype(
        jnp.float32
    )
    gate_value = jnp.sum(probability * chosen_mask, axis=-1)
    arrived_rows = to_owner(pack(routed))
    before = jnp.einsum(
        "sjcw,jwf->sjcf", arrived_rows, expert_in, preferred_element_type=jnp.float32
    )
    hidden = jax.nn.gelu(before, approximate=True).astype(jnp.bfloat16)
    outcome_part = jnp.einsum(
        "sjcf,jfw->sjcw", hidden, expert_out, preferred_element_type=jnp.float32
    )
    expert_rows = unpack(to_home(outcome_part))
    result = (middle + gate_value[:, None] * expert_rows.astype(jnp.float32)).astype(jnp.bfloat16)
    upstream = cotangent.astype(jnp.float32)
    row_grads = (gate_value[:, None] * upstream).astype(jnp.bfloat16)
    arrived_grads = to_owner(pack(row_grads))
    out_gradient = jnp.einsum(
        "sjcf,sjcw->jfw", hidden, arrived_grads, preferred_element_type=jnp.float32
    )
    hidden_grad = jnp.einsum(
        "sjcw,jfw->sjcf", arrived_grads, expert_out, preferred_element_type=jnp.float32
    )
    gelu_pull = jax.vjp(lambda pre_act: jax.nn.gelu(pre_act, approximate=True), before)[1]
    before_grad = gelu_pull(hidden_grad)[0].astype(jnp.bfloat16)
    in_gradient = jnp.einsum(
        "sjcw,sjcf->jwf", arrived_rows, before_grad, preferred_element_type=jnp.float32
    )
    rows_part = jnp.einsum(
        "sjcf,jwf->sjcw", before_grad, expert_in, preferred_element_type=jnp.float32
    )
    routed_rows_grad = unpack(to_home(rows_part))
    gate_grad = jnp.sum(upstream * expert_rows.astype(jnp.float32), axis=-1)
    logit_grad = ((gate_grad * gate_value)[:, None] * (chosen_mask - probability)).astype(
        jnp.bfloat16
    )
    router_grad = jnp.einsum("tw,te->we", routed, logit_grad, preferred_element_type=jnp.float32)
    routed_grad = jnp.einsum(
        "te,we->tw", logit_grad, router_weight, preferred_element_type=jnp.float32
    )
    routed_grad = routed_grad + routed_rows_grad.astype(jnp.float32)
    middle_part, expert_gain_grad = second_pull(routed_grad)
    middle_grad = upstream + middle_part
    attention_grad = middle_grad.astype(jnp.bfloat16)
    output_grad = jnp.einsum("tk,tw->kw", mixed, attention_grad, preferred_element_type=jnp.float32)
    mixed_grad = jnp.einsum(
        "tw,kw->tk", attention_grad, output_weight, preferred_element_type=jnp.float32
    )
    mixed_grad_heads = mixed_grad.astype(jnp.bfloat16).reshape(length, heads_here, head_size)

    def backward_block(running, packed):
        key_total, value_total, table_total = running
        first_row, log_total = packed
        scores, indicator, query_block = scores_at(first_row)
        weights_full = jnp.exp(scores - log_total[:, :, None])
        grad_block = lax.dynamic_slice_in_dim(mixed_grad_heads, first_row, block_rows, 0)
        value_total = value_total + jnp.einsum(
            "hrk,rhd->khd",
            weights_full.astype(jnp.bfloat16),
            grad_block,
            preferred_element_type=jnp.float32,
        )
        weight_grad = jnp.einsum(
            "rhd,khd->hrk", grad_block, value_heads, preferred_element_type=jnp.float32
        )
        score_grad = weights_full * (
            weight_grad - jnp.sum(weights_full * weight_grad, axis=-1, keepdims=True)
        )
        score_grad = score_grad.astype(jnp.bfloat16)
        table_total = table_total + jnp.einsum(
            "hrk,rkb->bh", score_grad, indicator, preferred_element_type=jnp.float32
        )
        query_block_grad = (
            jnp.einsum("hrk,khd->rhd", score_grad, key_heads, preferred_element_type=jnp.float32)
            * 0.125
        )
        key_total = (
            key_total
            + jnp.einsum(
                "hrk,rhd->khd", score_grad, query_block, preferred_element_type=jnp.float32
            )
            * 0.125
        )
        return ((key_total, value_total, table_total), query_block_grad.astype(jnp.bfloat16))

    zero_heads = jnp.zeros((length, heads_here, head_size), jnp.float32)
    zero_table = jnp.zeros((buckets, heads_here), jnp.float32)
    final_state, query_blocks = lax.scan(
        backward_block, (zero_heads, zero_heads, zero_table), (starts, log_totals)
    )
    key_total, value_total, table_grad = final_state
    query_grad = query_blocks.reshape(length, heads_here * head_size)
    key_grad = key_total.reshape(length, heads_here * head_size).astype(jnp.bfloat16)
    value_grad = value_total.reshape(length, heads_here * head_size).astype(jnp.bfloat16)
    query_weight_grad = jnp.einsum(
        "tw,tk->wk", normed, query_grad, preferred_element_type=jnp.float32
    )
    key_weight_grad = jnp.einsum("tw,tk->wk", normed, key_grad, preferred_element_type=jnp.float32)
    value_weight_grad = jnp.einsum(
        "tw,tk->wk", normed, value_grad, preferred_element_type=jnp.float32
    )
    normed_part = jnp.einsum(
        "tk,wk->tw", query_grad, query_weight, preferred_element_type=jnp.float32
    )
    normed_part = normed_part + jnp.einsum(
        "tk,wk->tw", key_grad, key_weight, preferred_element_type=jnp.float32
    )
    normed_part = normed_part + jnp.einsum(
        "tk,wk->tw", value_grad, value_weight, preferred_element_type=jnp.float32
    )
    normed_grad = over_heads(normed_part)
    input_part, attention_gain_grad = first_pull(normed_grad)
    input_gradient = middle_grad + input_part
    summed = lax.psum(
        (
            query_weight_grad,
            key_weight_grad,
            value_weight_grad,
            output_grad,
            table_grad,
            router_grad,
            attention_gain_grad,
            expert_gain_grad,
        ),
        "expert",
    )
    return (
        result,
        input_gradient,
        summed[6],
        summed[0],
        summed[1],
        summed[2],
        summed[3],
        summed[4],
        summed[7],
        summed[5],
        in_gradient,
        out_gradient,
    )


def solution(mesh):
    placed = (
        P("expert", None),
        P("expert", None),
        P("expert"),
        P("expert"),
        P(),
        P(),
        P(None, "shard"),
        P(None, "shard"),
        P(None, "shard"),
        P("shard", None),
        P(None, "shard"),
        P(),
        P(),
        P("expert", None, "shard"),
        P("expert", "shard", None),
    )
    return jax.shard_map(
        on_device,
        mesh=mesh,
        in_specs=placed,
        out_specs=(
            P("expert", None),
            P("expert", None),
            P(),
            P(None, "shard"),
            P(None, "shard"),
            P(None, "shard"),
            P("shard", None),
            P(None, "shard"),
            P(),
            P(),
            P("expert", None, "shard"),
            P("expert", "shard", None),
        ),
        check_vma=False,
    )
```

profile of v0, /device:TPU:0, one launch (start us, length us, event | category | flops | bytes accessed | tf_op | source)
XLA Modules:
  0.0 1266.0 jit_solution(5977565976954976773)
XLA Ops:
  15.3 126.8 %while.30 = (s32[]{:T(128)}, bf16[2,512,3,64]{1,3,2,0:T(8,128)(2,1)S(1)}, f32[2,3,512]{2,1,0:T(4,128)S(1)}, s32[2]{0:T(128)S(1)}, bf16[1024,3,64]{0,2,1:T(8,128)...) while((s32[]{:T(128)}, ...), condition=%wide.region_5.6_spmd.clone, body=%wide.region_1.5_spmd.clone.sunk | while | flops 737245696 | bytes 114486016 | solution.py:118
  19.7 16.1 %fusion.177 = f32[9,512,1024]{2,0,1:T(8,128)} fusion(s32[512,1024]{1,0:T(8,128)S(1)} %constant_dynamic-slice_fusion.4, bf16[32,9]{0,1:T(8,128)(2,1)S(1)} %get-tuple-element.482), kind=kOutput, calls=%fused_computation.10.clone.1 | convolution fusion | flops 318767104 | bytes 20972096 | tf_op jit(solution)/shard_map/while/body/eval_jaxpr/rkb,bc->crk/dot_general | solution.py:97
  35.8 23.4 %copy.45 = f32[9,512,1024]{2,1,0:T(8,128)} copy(f32[9,512,1024]{2,0,1:T(8,128)} %fusion.177) | data formatting | bytes 37748736 | tf_op jit(solution)/shard_map/while/body/eval_jaxpr/rkb,bc->crk/dot_general | solution.py:97
  59.3 12.1 reduce_sum.162
  83.0 16.1 %fusion.177 = f32[9,512,1024]{2,0,1:T(8,128)} fusion(s32[512,1024]{1,0:T(8,128)S(1)} %constant_dynamic-slice_fusion.4, bf16[32,9]{0,1:T(8,128)(2,1)S(1)} %get-tuple-element.482), kind=kOutput, calls=%fused_computation.10.clone.1 | convolution fusion | flops 318767104 | bytes 20972096 | tf_op jit(solution)/shard_map/while/body/eval_jaxpr/rkb,bc->crk/dot_general | solution.py:97
  99.1 23.4 %copy.45 = f32[9,512,1024]{2,1,0:T(8,128)} copy(f32[9,512,1024]{2,0,1:T(8,128)} %fusion.177) | data formatting | bytes 37748736 | tf_op jit(solution)/shard_map/while/body/eval_jaxpr/rkb,bc->crk/dot_general | solution.py:97
  122.6 12.1 reduce_sum.162
  146.8 4.3 scatter_custom_fusion
  151.3 66.2 %all-reduce.12.cloned.1.call-done = f32[1024,768]{1,0:T(8,128)} async-done(((f32[1024,768]{1,0:T(8,128)}), f32[1024,768]{1,0:T(8,128)}) %all-reduce.12.cloned.1.call-update) | async-done | bytes 3145744 | tf_op jit(solution)/shard_map/psum | solution.py:77
  223.1 5.6 gather_fusion
  228.7 5.6 all-to-all-start
  237.4 5.6 gather_fusion.2
  243.0 45.2 %all-to-all-done = bf16[8,192,768]{2,1,0:T(8,128)(2,1)} async-done(((bf16[8,192,768]{2,1,0:T(8,128)(2,1)}), bf16[8,192,768]{2,1,0:T(8,128)(2,1)}, u32[]{:S(2)}, u32[]{:S(2)}) %all-to-all-start) | async-done | bytes 2359328 | tf_op jit(solution)/shard_map/all_to_all | solution.py:65
  298.7 5.1 fusion.67
  303.8 42.6 %all-to-all-done.2 = bf16[8,192,768]{2,1,0:T(8,128)(2,1)S(1)} async-done(((bf16[8,192,768]{2,1,0:T(8,128)(2,1)}), bf16[8,192,768]{2,1,0:T(8,128)(2,1)S(1)}, u32[]{:S(2)}, u32[]{:S(2)}) %all-to-all-start.2) | async-done | bytes 2359328 | tf_op jit(solution)/shard_map/all_to_all | solution.py:65
  346.3 6.9 fusion.45
  354.7 4.2 fusion.63
  358.9 163.1 %all-reduce.17 = (bf16[8,192,768]{2,1,0:T(8,128)(2,1)}, bf16[8,192,768]{2,1,0:T(8,128)(2,1)S(1)}) all-reduce(f32[8,192,768]{2,1,0:T(8,128)} %fusion.67, f32[8,192,768]{2,1,0:T(8,128)} %fusion.63), channel_id=1, replica_groups=mesh['expert'=8,'shard'=4] {'shard'}, use_global_device_ids=true, to_apply=%region_12.13 | all-reduce | flops 2359296 | bytes 14155776 | tf_op jit(solution)/shard_map/psum | solution.py:70
  522.0 58.6 %all_to_all.20 = bf16[8,192,768]{2,1,0:T(8,128)(2,1)} all-to-all(bf16[8,192,768]{2,1,0:T(8,128)(2,1)S(1)} %get-tuple-element.293), channel_id=1, replica_groups=mesh['expert'=8,'shard'=4] {'expert'}, dimensions={0} | all-to-all | bytes 4718592 | tf_op jit(solution)/shard_map/all_to_all | solution.py:71
  580.6 4.4 all-to-all-start.1
  586.9 5.2 gather_fusion.3
  592.1 46.4 %all-to-all-done.1 = bf16[8,192,768]{2,1,0:T(8,128)(2,1)} async-done(((bf16[8,192,768]{2,1,0:T(8,128)(2,1)}), bf16[8,192,768]{2,1,0:T(8,128)(2,1)}, u32[]{:S(2)}, u32[]{:S(2)}) %all-to-all-start.1) | async-done | bytes 2359328 | tf_op jit(solution)/shard_map/all_to_all | solution.py:71
  640.4 5.2 gather_fusion.1
  658.1 405.9 %while.31 = (s32[]{:T(128)}, f32[1024,3,64]{0,2,1:T(8,128)S(1)}, f32[1024,3,64]{0,2,1:T(8,128)}, f32[32,3]{0,1:T(4,128)S(1)}, bf16[2,512,3,64]{1,3,2,0:T(8,128)(...) while((s32[]{:T(128)}, f32[1024,3,64]{0,2,1:T(8,128)S(1)}, ...), condition=%wide.region_19.20_spmd.clone, body=%wide.region_16.19_spmd.clone.sunk | while | flops 1444543232 | bytes 269584096 | solution.py:213
  666.0 4.9 fusion.194
  671.0 12.3 iota_compare_fusion.9
  683.2 90.0 %copy.47 = pred[512,1024,32]{1,2,0:T(32,128)(4,1)} copy(pred[512,1024,32]{0,2,1:T(32,128)(4,1)} %iota_compare_fusion.9) | data formatting | bytes 33554432 | tf_op jit(solution)/shard_map/while/body/eval_jaxpr/eq | solution.py:96
  773.2 19.4 %convolution_bitcast_fusion.3 = f32[9,512,1024]{2,0,1:T(8,128)} fusion(pred[512,1024,32]{1,2,0:T(32,128)(4,1)} %copy.47, bf16[32,9]{0,1:T(8,128)(2,1)S(1)} %get-tuple-element.531), kind=kOutput, calls=%fused_computation.25.clone.1 | convolution fusion | flops 301989888 | bytes 35652160 | tf_op jit(solution)/shard_map/while/body/eval_jaxpr/rkb,bc->crk/dot_general | solution.py:97
  792.6 23.4 %copy.48 = f32[9,512,1024]{2,1,0:T(8,128)} copy(f32[9,512,1024]{2,0,1:T(8,128)} %convolution_bitcast_fusion.3) | data formatting | bytes 37748736 | tf_op jit(solution)/shard_map/while/body/eval_jaxpr/rkb,bc->crk/dot_general | solution.py:97
  816.1 12.1 reduce_sum.164
  828.2 6.0 multiply_reduce_fusion.5
  841.5 7.6 copy.49
  849.1 12.0 fusion.197
  868.8 4.9 fusion.194
  873.7 12.3 iota_compare_fusion.9
  886.0 90.0 %copy.47 = pred[512,1024,32]{1,2,0:T(32,128)(4,1)} copy(pred[512,1024,32]{0,2,1:T(32,128)(4,1)} %iota_compare_fusion.9) | data formatting | bytes 33554432 | tf_op jit(solution)/shard_map/while/body/eval_jaxpr/eq | solution.py:96
  976.0 19.4 %convolution_bitcast_fusion.3 = f32[9,512,1024]{2,0,1:T(8,128)} fusion(pred[512,1024,32]{1,2,0:T(32,128)(4,1)} %copy.47, bf16[32,9]{0,1:T(8,128)(2,1)S(1)} %get-tuple-element.531), kind=kOutput, calls=%fused_computation.25.clone.1 | convolution fusion | flops 301989888 | bytes 35652160 | tf_op jit(solution)/shard_map/while/body/eval_jaxpr/rkb,bc->crk/dot_general | solution.py:97
  995.4 23.4 %copy.48 = f32[9,512,1024]{2,1,0:T(8,128)} copy(f32[9,512,1024]{2,0,1:T(8,128)} %convolution_bitcast_fusion.3) | data formatting | bytes 37748736 | tf_op jit(solution)/shard_map/while/body/eval_jaxpr/rkb,bc->crk/dot_general | solution.py:97
  1018.9 12.1 reduce_sum.164
  1031.0 6.0 multiply_reduce_fusion.5
  1044.2 7.6 copy.49
  1051.8 12.0 fusion.197
  1076.7 5.3 fusion.72
  1082.0 6.5 fusion.69
  1088.9 47.9 %all-reduce.14.cloned.1.call-done = f32[1024,768]{1,0:T(8,128)} async-done(((f32[1024,768]{1,0:T(8,128)}), f32[1024,768]{1,0:T(8,128)}) %all-reduce.14.cloned.1.call-update) | async-done | bytes 3145744 | tf_op jit(solution)/shard_map/psum | solution.py:77
  1139.8 39.8 %all-reduce.4 = (f32[768]{0:T(1024)}, f32[32,3]{0,1:T(4,128)}, f32[768]{0:T(1024)}, f32[768,8]{0,1:T(8,128)}) all-reduce(f32[768]{0:T(1024)S(1)} %get-tuple-element.238, f32[32,3]{0,1:T(4,128)S(1)} %get-tuple-element.145, f32[768]{0:T(1024)S(1)} %copy-done.75, ...), channel_id=1, replica_groups=mesh['expert'=8,'shard'=4] {'expert'}, use_global_device_ids=true, to_apply=%region_23.24 | all-reduce | flops 7776 | bytes 62208 | tf_op jit(solution)/shard_map/psum | solution.py:239
  1179.6 5.6 fusion.58
  1185.2 67.3 %all-reduce.16.cloned.1.call-done = (f32[768,192]{0,1:T(8,128)}, f32[768,192]{0,1:T(8,128)}, f32[768,192]{0,1:T(8,128)}, f32[192,768]{1,0:T(8,128)}) async-done(((f32[768,192]{0,1:T(8,128)}, f32[768,192]{0,1:T(8,128)}, f32[768,192]{0,1:T(8,128)}, f32[192,768]{1,0:T(8,128)}), (f32[768,192]{0,1:T(8,128)}, f32[768,192]{0,1:T(8,128)}, f32[768,192]{0,1:T(8,128)}, ...) | async-done | bytes 2359312 | tf_op jit(solution)/shard_map/psum | solution.py:239
  (275 shorter events, 116.9 us)
Async XLA Ops:
  7.2 291.5 %copy-start = (bf16[1,768,768]{2,1,0:T(8,128)(2,1)S(1)}, bf16[1,768,768]{2,1,0:T(8,128)(2,1)}, u32[]{:S(2)}) copy-start(bf16[1,768,768]{2,1,0:T(8,128)(2,1)} %param.33) | copy-start | bytes 3538948
  7.2 6.0 copy-start.41
  7.2 210.2 %all-reduce.12.cloned.1.call-start = ((), (), s32[]{:S(2)}) async-start(), calls=%async_computation.4 | async-start | bytes 6291456 | tf_op jit(solution)/shard_map/psum | solution.py:77
  9.4 4.5 copy-start.45
  15.3 128.5 %copy-start.33 = (bf16[192,768]{1,0:T(8,128)(2,1)S(1)}, bf16[192,768]{1,0:T(8,128)(2,1)}, u32[]{:S(2)}) copy-start(bf16[192,768]{1,0:T(8,128)(2,1)} %param.28) | copy-start | bytes 884740
  142.2 3.9 copy-start.3
  143.8 73.6 %copy-start.9 = (bf16[1024,768]{1,0:T(8,128)(2,1)S(1)}, bf16[1024,768]{1,0:T(8,128)(2,1)}, u32[]{:S(2)}) copy-start(bf16[1024,768]{1,0:T(8,128)(2,1)} %param.19) | copy-start | bytes 4718596
  151.3 70.2 %copy-start.72 = (f32[768]{0:T(1024)S(1)}, f32[768]{0:T(1024)}, u32[]{:S(2)}) copy-start(f32[768]{0:T(1024)} %param.30) | copy-start | bytes 9220
  228.7 5.7 copy-start.17
  228.7 5.7 copy-start.63
  228.7 59.5 %all-to-all-start = ((bf16[8,192,768]{2,1,0:T(8,128)(2,1)}), bf16[8,192,768]{2,1,0:T(8,128)(2,1)}, u32[]{:S(2)}, u32[]{:S(2)}) async-start(bf16[8,192,768]{2,1,0:T(8,128)(2,1)} %bitcast.234), calls=%async_computation | async-start | bytes 4718592 | tf_op jit(solution)/shard_map/all_to_all | solution.py:65
  234.9 413.2 %copy-start.47 = (f32[1024]{0:T(1024)}, f32[1024]{0:T(1024)S(1)}, u32[]{:S(2)}) copy-start(f32[1024]{0:T(1024)S(1)} %get-tuple-element.304) | copy-start | bytes 12292
  288.2 58.1 %all-to-all-start.2 = ((bf16[8,192,768]{2,1,0:T(8,128)(2,1)}), bf16[8,192,768]{2,1,0:T(8,128)(2,1)S(1)}, u32[]{:S(2)}, u32[]{:S(2)}) async-start(bf16[8,192,768]{2,1,0:T(8,128)(2,1)} %bitcast.235), calls=%async_computation.2 | async-start | bytes 4718592 | tf_op jit(solution)/shard_map/all_to_all | solution.py:65
  346.3 6.9 copy-start.29
  346.3 8.3 copy-start.78
  580.6 57.9 %all-to-all-start.1 = ((bf16[8,192,768]{2,1,0:T(8,128)(2,1)}), bf16[8,192,768]{2,1,0:T(8,128)(2,1)}, u32[]{:S(2)}, u32[]{:S(2)}) async-start(bf16[8,192,768]{2,1,0:T(8,128)(2,1)} %get-tuple-element.292), calls=%async_computation.1 | async-start | bytes 4718592 | tf_op jit(solution)/shard_map/all_to_all | solution.py:71
  585.0 551.8 %all-reduce.14.cloned.1.call-start = ((), (), s32[]{:S(2)}) async-start(), calls=%async_computation.5 | async-start | bytes 6291456 | tf_op jit(solution)/shard_map/psum | solution.py:77
  640.3 7.8 copy-start.62
  640.3 7.8 copy-start.36
  640.3 7.8 copy-start.64
  648.4 3.5 copy-start.68
  651.9 3.9 copy-start.34
  654.2 3.9 copy-start.4
  654.2 3.9 copy-start.40
  654.2 3.9 copy-start.50
  654.2 3.9 copy-start.77
  654.2 3.9 copy-start.80
  816.1 12.1 copy-start.20
  834.2 4.0 copy-start.11
  834.2 4.0 copy-start.21
  1018.9 12.1 copy-start.20
  1037.0 4.0 copy-start.11
  1037.0 4.0 copy-start.21
  1069.5 183.0 %all-reduce.16.cloned.1.call-start = ((), (), s32[]{:S(2)}) async-start(), calls=%async_computation.6 | async-start | bytes 4718592 | tf_op jit(solution)/shard_map/psum | solution.py:239
  1076.7 5.3 copy-start.30
  1082.0 6.6 copy-start.18
  1082.0 6.6 copy-start.37
  1082.0 6.6 copy-start.48
  1082.0 6.6 copy-start.55
  1082.0 6.6 copy-start.58
  1082.0 6.6 copy-start.69
  1082.0 54.8 %copy-start.10 = (bf16[1024,768]{1,0:T(8,128)(2,1)S(1)}, bf16[1024,768]{1,0:T(8,128)(2,1)}, u32[]{:S(2)}) copy-start(bf16[1024,768]{1,0:T(8,128)(2,1)} %param.19) | copy-start | bytes 4718596
  1082.0 54.8 %copy-start.52 = (f32[1024]{0:T(1024)S(1)}, f32[1024]{0:T(1024)}, u32[]{:S(2)}) copy-start(f32[1024]{0:T(1024)} %copy-done.51) | copy-start | bytes 12292
  1082.0 54.8 %copy-start.67 = (f32[768]{0:T(1024)S(1)}, f32[768]{0:T(1024)}, u32[]{:S(2)}) copy-start(f32[768]{0:T(1024)} %param.24) | copy-start | bytes 9220
  1088.6 51.2 %copy-start.75 = (f32[768]{0:T(1024)S(1)}, f32[768]{0:T(1024)}, u32[]{:S(2)}) copy-start(f32[768]{0:T(1024)} %get-tuple-element.236) | copy-start | bytes 9220
  1088.6 91.0 %copy-start.71 = (f32[1024]{0:T(1024)S(1)}, f32[1024]{0:T(1024)}, u32[]{:S(2)}) copy-start(f32[1024]{0:T(1024)} %copy-done.70) | copy-start | bytes 12292
  1179.6 79.5 %copy-start.1 = (bf16[1,768,768]{2,1,0:T(8,128)(2,1)S(1)}, bf16[1,768,768]{2,1,0:T(8,128)(2,1)}, u32[]{:S(2)}) copy-start(bf16[1,768,768]{2,1,0:T(8,128)(2,1)} %param.33) | copy-start | bytes 3538948
  1252.5 5.8 copy-start.38
  (47 other events, 94.2 us)
Sparse Core Ops, SparseCore 0:
  146.3 71.1 all-reduce.11
  1069.6 67.0 all-reduce.13
  1141.3 111.1 all-reduce.15
where the time goes:
time: 1280 us; the launch traced here: 1270 us
  local copies, waits for them, and re-layouts  358 us (28%)
  waiting for transfers between devices  315 us (25%)
  blocking collectives  262 us (20%)
  matrix products  184 us (14%)
  other arithmetic  108 us (8%)
  between operations  15.1 us (1%)
  starting transfers between devices  14.3 us (1%)
    eq x2, local copies, waits for them, and re-layouts, scores_at(): bucket_block[:, :, None] == bucket_range[None, None, :]  180 us
    psum x1, blocking collectives, to_home(): summed = lax.psum(merged, 'shard')  163 us
    psum x2, waiting for transfers between devices, over_heads(): return lax.psum(partial_sums, 'shard')  114 us
    dot_general x4, local copies, waits for them, and re-layouts, scores_at(): jnp.einsum('rkb,bc->crk', indicator, split_table, preferred_element_type=...  93.8 us
    all_to_all x2, waiting for transfers between devices, to_owner(): lax.all_to_all(buffer, 'expert', split_axis=0, concat_axis=0, tiled=True)  87.7 us
    dot_general x4, matrix products, scores_at(): jnp.einsum('rkb,bc->crk', indicator, split_table, preferred_element_type=...  71 us
    psum x1, waiting for transfers between devices, on_device(): lax.psum((query_weight_grad, key_weight_grad, value_weight_grad, output_g...  67.3 us
    all_to_all x1, blocking collectives, to_home(): lax.all_to_all(summed.astype(jnp.bfloat16), 'expert', split_axis=0, conca...  58.6 us
  transfers between devices with their start and end apart: 6, of which 6 were waited for; matrix products, arithmetic and copies ran while one was open for 4% of the time, Pallas kernels for 0%

commit v1 on v0

v1 whole, which is shorter than its diff:
```python
import functools
import jax
import jax.numpy as jnp
from jax import lax
from jax.experimental import pallas as pl
from jax.experimental.pallas import tpu as pltpu
from jax.sharding import PartitionSpec as P

VMEM_LIMIT = 56 * 1024 * 1024


def dot(a, b, ca=1, cb=0):
    return lax.dot_general(a, b, (((ca,), (cb,)), ((), ())), preferred_element_type=jnp.float32)


def bias_strip(values_row, rows):
    total = values_row.shape[-1]
    wide = jnp.broadcast_to(values_row.reshape(1, total), (rows, total))
    return pltpu.roll(wide, total - rows + 1, 1, stride=1, stride_axis=0)


def attention_forward_kernel(heads, head_size, rows, in_ref, gain_ref, wq_ref, wk_ref, wv_ref, bias_ref, mixed_ref, qkv_ref, normed_ref, strip_ref):
    length = in_ref.shape[0]
    blocks = length // rows
    hd = heads * head_size
    source = in_ref[...].astype(jnp.float32)
    inverse = lax.rsqrt(jnp.mean(source * source, axis=1, keepdims=True) + 1e-06)
    normed_ref[...] = (source * inverse * gain_ref[...]).astype(jnp.bfloat16)
    for at, ref in enumerate((wq_ref, wk_ref, wv_ref)):
        qkv_ref[at * hd : (at + 1) * hd, :] = dot(ref[...], normed_ref[...], 0, 1).astype(jnp.bfloat16)
    for h in range(heads):
        strip_ref[...] = bias_strip(bias_ref[h : h + 1, :], rows)
        q = (qkv_ref[h * head_size : (h + 1) * head_size, :].astype(jnp.float32) * 0.125).T.astype(jnp.bfloat16)
        kt = qkv_ref[hd + h * head_size : hd + (h + 1) * head_size, :]
        vt = qkv_ref[2 * hd + h * head_size : 2 * hd + (h + 1) * head_size, :]
        for i in range(blocks):
            s = dot(q[i * rows : (i + 1) * rows], kt)
            at = (blocks - 1 - i) * rows
            s = s + strip_ref[:, at : at + length]
            peak = jnp.max(s, axis=1, keepdims=True)
            p = jnp.exp(s - peak)
            total = jnp.sum(p, axis=1, keepdims=True)
            o = dot(p.astype(jnp.bfloat16), vt, 1, 1) / total
            mixed_ref[h * head_size : (h + 1) * head_size, i * rows : (i + 1) * rows] = o.T.astype(jnp.bfloat16)


def in_vmem(count):
    return [pl.BlockSpec(memory_space=pltpu.VMEM)] * count


def attention_forward(inputs, gain, wq, wk, wv, bias_values, heads, head_size, rows=256):
    length = inputs.shape[0]
    hd = heads * head_size
    return pl.pallas_call(
        functools.partial(attention_forward_kernel, heads, head_size, rows),
        out_shape=(
            jax.ShapeDtypeStruct((hd, length), jnp.bfloat16),
            jax.ShapeDtypeStruct((3 * hd, length), jnp.bfloat16),
            jax.ShapeDtypeStruct(inputs.shape, jnp.bfloat16),
        ),
        in_specs=in_vmem(6),
        out_specs=tuple(in_vmem(3)),
        scratch_shapes=[pltpu.VMEM((rows, bias_values.shape[1]), jnp.float32)],
        compiler_params=pltpu.CompilerParams(vmem_limit_bytes=VMEM_LIMIT),
        cost_estimate=pl.CostEstimate(flops=10**10, bytes_accessed=10**7, transcendentals=heads * length * length),
        name="attention_forward",
    )(inputs, gain, wq, wk, wv, bias_values)


def call(body, out_shape, args, name, flops, scratch=(), transcendentals=0):
    return pl.pallas_call(
        body,
        out_shape=out_shape,
        in_specs=in_vmem(len(args)),
        out_specs=jax.tree.map(lambda _: in_vmem(1)[0], out_shape),
        scratch_shapes=list(scratch),
        compiler_params=pltpu.CompilerParams(vmem_limit_bytes=VMEM_LIMIT),
        cost_estimate=pl.CostEstimate(flops=flops, bytes_accessed=10**7, transcendentals=transcendentals),
        name=name,
    )(*args)


def shape(dims, dtype=jnp.bfloat16):
    return jax.ShapeDtypeStruct(dims, dtype)


def join(refs, target):
    at = 0
    for ref in refs:
        target[at : at + ref.shape[0], :] = ref[...]
        at += ref.shape[0]


def route_tokens(mixed_pieces, ow_pieces, source, pack, gain, router, sizes):
    shards = len(mixed_pieces)
    tokens, width = source.shape

    def body(*refs):
        mixed_refs, ow_refs = refs[:shards], refs[shards : 2 * shards]
        source_ref, pack_ref, gain_ref, router_ref = refs[2 * shards : 2 * shards + 4]
        middle_ref, routed_ref, probability_ref = refs[2 * shards + 4 : 2 * shards + 7]
        middle = source_ref[...]
        for m, o in zip(mixed_refs, ow_refs):
            middle = middle + dot(m[...], o[...])
        middle_ref[...] = middle
        spread = lax.rsqrt(jnp.mean(middle * middle, axis=1, keepdims=True) + 1e-06)
        routed = (middle * spread * gain_ref[...]).astype(jnp.bfloat16)
        routed_ref[...] = routed
        packed = dot(pack_ref[...], routed).astype(jnp.bfloat16)
        at = 0
        for ref in refs[2 * shards + 7 :]:
            ref[...] = packed[at : at + ref.shape[0], :]
            at += ref.shape[0]
        logits = dot(routed, router_ref[...])
        powered = jnp.exp(logits - jnp.max(logits, axis=1, keepdims=True))
        probability_ref[...] = powered / jnp.sum(powered, axis=1, keepdims=True)

    out = (shape((tokens, width), jnp.float32), shape((tokens, width)), shape((tokens, router.shape[1]), jnp.float32))
    out = out + tuple(shape((n, width)) for n in sizes)
    args = (*mixed_pieces, *ow_pieces, source, pack, gain, router)
    return call(body, out, args, "route_tokens", 10**9)


def expert_forward(pieces, grads, router, mine, w_in, w_out):
    count, width = grads.shape
    n, k_all = len(pieces), len(w_in)

    def body(*refs):
        piece_refs = refs[:n]
        grads_ref, router_ref, mine_ref = refs[n : n + 3]
        in_refs, out_refs = refs[n + 3 : n + 3 + k_all], refs[n + 3 + k_all : n + 3 + 2 * k_all]
        slope_ref, both_ref = refs[n + 3 + 2 * k_all : n + 5 + 2 * k_all]
        join(piece_refs, both_ref)
        rows = both_ref[:count, :]
        logits = dot(rows, router_ref[...])
        powered = jnp.exp(logits - jnp.max(logits, axis=1, keepdims=True))
        gate = jnp.sum(powered * mine_ref[...], axis=1, keepdims=True) / jnp.sum(powered, axis=1, keepdims=True)
        both_ref[count:, :] = (gate * grads_ref[...].astype(jnp.float32)).astype(jnp.bfloat16)
        total = jnp.zeros((count, width), jnp.float32)
        for k in range(k_all):
            value, slope = gelu_pair(dot(rows, in_refs[k][...]))
            slope_ref[:, k * width : (k + 1) * width] = slope.astype(jnp.bfloat16)
            total = total + dot(value.astype(jnp.bfloat16), out_refs[k][...])
        total = total.astype(jnp.bfloat16)
        at = 0
        for ref in refs[n + 5 + 2 * k_all :]:
            ref[...] = total[at : at + ref.shape[0], :]
            at += ref.shape[0]

    out = (shape((count, k_all * width)), shape((2 * count, width))) + tuple(shape(p.shape) for p in pieces)
    args = (*pieces, grads, router, mine, *w_in, *w_out)
    return call(body, out, args, "expert_forward", 4 * 10**9, transcendentals=count * 4 * width)


def expert_backward(both, slope, w_in, w_out, sizes):
    count, width = slope.shape[0], both.shape[1]
    k_all = len(w_in)

    def body(both_ref, slope_ref, *refs):
        in_refs, out_refs = refs[:k_all], refs[k_all : 2 * k_all]
        grads = both_ref[count:, :]
        total = jnp.zeros((count, width), jnp.float32)
        for k in range(k_all):
            part_slope = slope_ref[:, k * width : (k + 1) * width].astype(jnp.float32)
            before_grad = (dot(grads, out_refs[k][...], 1, 1) * part_slope).astype(jnp.bfloat16)
            total = total + dot(before_grad, in_refs[k][...], 1, 1)
        total = total.astype(jnp.bfloat16)
        at = 0
        for ref in refs[2 * k_all :]:
            ref[...] = total[at : at + ref.shape[0], :]
            at += ref.shape[0]

    out = tuple(shape((n, width)) for n in sizes)
    return call(body, out, (both, slope, *w_in, *w_out), "expert_backward", 4 * 10**9)


def token_grads(back_rows, back_grads, pack_t, middle, routed, probability, chosen, grad, gain, router, ow_pieces):
    tokens, width = middle.shape
    n, shards = len(back_rows), len(ow_pieces)
    hd = ow_pieces[0].shape[0]

    def body(*refs):
        row_refs, grad_refs = refs[:n], refs[n : 2 * n]
        pack_ref, middle_ref, routed_ref, probability_ref, chosen_ref, g_ref, gain_ref, router_ref = refs[2 * n : 2 * n + 8]
        ow_refs = refs[2 * n + 8 : 2 * n + 8 + shards]
        token_ref, router_part_ref, gain_part_ref = refs[2 * n + 8 + shards : 2 * n + 11 + shards]
        mixed_refs = refs[2 * n + 11 + shards : 2 * n + 11 + 2 * shards]
        buffer = refs[-1]
        g = g_ref[...].astype(jnp.float32)
        middle = middle_ref[...]
        chosen = chosen_ref[...]
        probability = probability_ref[...]
        gate = jnp.sum(probability * chosen, axis=1, keepdims=True)
        join(row_refs, buffer)
        rows = dot(pack_ref[...], buffer[...])
        token_ref[:, :width] = (middle + gate * rows).astype(jnp.bfloat16)
        gate_grad = jnp.sum(g * rows, axis=1, keepdims=True)
        logit_grad = (gate_grad * gate * (chosen - probability)).astype(jnp.bfloat16)
        router_part_ref[...] = dot(routed_ref[...], logit_grad, 0, 0)
        join(grad_refs, buffer)
        routed_grad = dot(logit_grad, router_ref[...], 1, 1) + dot(pack_ref[...], buffer[...])
        spread = lax.rsqrt(jnp.mean(middle * middle, axis=1, keepdims=True) + 1e-06)
        gain_part_ref[...] = jnp.sum(routed_grad * middle * spread, axis=0, keepdims=True)
        u = routed_grad * gain_ref[...]
        mean = jnp.mean(u * middle, axis=1, keepdims=True)
        middle_grad = (g + spread * u - middle * (spread * spread * spread * mean)).astype(jnp.bfloat16)
        token_ref[:, width:] = middle_grad
        for m, o in zip(mixed_refs, ow_refs):
            m[...] = dot(middle_grad, o[...], 1, 1).astype(jnp.bfloat16)

    out = (
        shape((tokens, 2 * width)),
        shape((width, router.shape[1]), jnp.float32),
        shape((1, width), jnp.float32),
    ) + (shape((tokens, hd)),) * shards
    args = (*back_rows, *back_grads, pack_t, middle, routed, probability, chosen, grad, gain, router, *ow_pieces)
    scratch = [pltpu.VMEM((pack_t.shape[1], width), jnp.bfloat16)]
    return call(body, out, args, "token_grads", 2 * 10**9, scratch)


def first_parts(normed, head_grads, weights, high):
    length, width = normed.shape
    rows = head_grads[0].shape[0]
    columns = rows * len(head_grads)
    half = width // 2

    def body(high_ref, normed_ref, weights_ref, *refs):
        keep_ref, sent_ref, gain_ref, part = refs[len(head_grads) :]
        for i, ref in enumerate(refs[: len(head_grads)]):
            part[:, i * rows : (i + 1) * rows] = dot(normed_ref[...], ref[...], 0, 1)
        gain_ref[...] = jnp.sum(weights_ref[...].astype(jnp.float32) * part[...], axis=1, keepdims=True)
        bit = high_ref[0]
        keep_ref[...] = part[pl.ds(pl.multiple_of(bit * half, half), half), :]
        sent_ref[...] = part[pl.ds(pl.multiple_of((1 - bit) * half, half), half), :].astype(jnp.bfloat16)

    out = (shape((half, columns), jnp.float32), shape((half, columns)), shape((width, 1), jnp.float32))
    return with_bit(body, out, (normed, weights, *head_grads), high, "first_parts", [pltpu.VMEM((width, columns), jnp.float32)])


def with_bit(body, out, args, high, name, scratch=()):
    return pl.pallas_call(
        body,
        out_shape=out,
        in_specs=[pl.BlockSpec(memory_space=pltpu.SMEM)] + in_vmem(len(args)),
        out_specs=jax.tree.map(lambda _: in_vmem(1)[0], out),
        scratch_shapes=list(scratch),
        compiler_params=pltpu.CompilerParams(vmem_limit_bytes=VMEM_LIMIT),
        cost_estimate=pl.CostEstimate(flops=2 * 10**9, bytes_accessed=10**7, transcendentals=0),
        name=name,
    )(high, *args)


def last_parts(normed, head_grad, weights, gain_before, gain, middle_grad, mixed_t, small, high):
    length, width = normed.shape
    rows, hd = head_grad.shape[0], mixed_t.shape[0]
    columns = rows + hd + small.shape[1]
    half = width // 2

    def body(high_ref, normed_ref, head_ref, weights_ref, before_ref, gain_ref, middle_ref, mixed_ref, small_ref, keep_ref, sent_ref, part):
        head_part = dot(normed_ref[...], head_ref[...], 0, 1)
        part[:, :rows] = head_part
        part[:, rows : rows + hd] = dot(middle_ref[...], mixed_ref[...], 0, 1)
        total = before_ref[...] + jnp.sum(weights_ref[...].astype(jnp.float32) * head_part, axis=1, keepdims=True)
        lane = lax.broadcasted_iota(jnp.int32, small_ref.shape, 1)
        part[:, rows + hd :] = jnp.where(lane == 0, total / gain_ref[...], small_ref[...])
        bit = high_ref[0]
        keep_ref[...] = part[pl.ds(pl.multiple_of(bit * half, half), half), :]
        sent_ref[...] = part[pl.ds(pl.multiple_of((1 - bit) * half, half), half), :].astype(jnp.bfloat16)

    out = (shape((half, columns), jnp.float32), shape((half, columns)))
    args = (normed, head_grad, weights, gain_before, gain, middle_grad, mixed_t, small)
    return with_bit(body, out, args, high, "last_parts", [pltpu.VMEM((width, columns), jnp.float32)])


def place_sums(first, last, high_first, high_last, heads, head_size):
    half, wide = first[0].shape
    width = 2 * half
    hd = heads * head_size
    extra = last[0].shape[1] - 3 * head_size - hd

    def body(first_bit, last_bit, a0, a1, b0, b1, q_ref, k_ref, v_ref, o_ref, small_ref):
        for i, (own, other) in enumerate(((a0, a1), (b0, b1))):
            bit = (first_bit, last_bit)[i][0]
            for ref, place in ((own, bit), (other, 1 - bit)):
                at = pl.ds(pl.multiple_of(place * half, half), half)
                value = ref[...].astype(jnp.float32)
                count = wide // (3 * head_size) if i == 0 else 1
                for j in range(count):
                    h = j if i == 0 else heads - 1
                    for c, out_ref in enumerate((q_ref, k_ref, v_ref)):
                        start = (3 * j + c) * head_size
                        out_ref[at, h * head_size : (h + 1) * head_size] = value[:, start : start + head_size]
                if i == 1:
                    o_ref[:, at] = value[:, 3 * head_size : 3 * head_size + hd].T
                    small_ref[at, :] = value[:, 3 * head_size + hd :]

    out = (shape((width, hd), jnp.float32),) * 3 + (shape((hd, width), jnp.float32), shape((width, extra), jnp.float32))
    return pl.pallas_call(
        body,
        out_shape=out,
        in_specs=[pl.BlockSpec(memory_space=pltpu.SMEM)] * 2 + in_vmem(4),
        out_specs=tuple(in_vmem(5)),
        compiler_params=pltpu.CompilerParams(vmem_limit_bytes=VMEM_LIMIT),
        cost_estimate=pl.CostEstimate(flops=10**6, bytes_accessed=10**7, transcendentals=0),
        name="place_sums",
    )(high_first, high_last, *first, *last)


def expert_weights_kernel(shards, count, all_ref, wi_ref, wo_ref, in_ref, out_ref):
    for s in range(shards):
        rows = all_ref[2 * s * count : (2 * s + 1) * count, :]
        grads = all_ref[(2 * s + 1) * count : (2 * s + 2) * count, :]
        value, slope = gelu_pair(dot(rows, wi_ref[...]))
        before_grad = (dot(grads, wo_ref[...], 1, 1) * slope).astype(jnp.bfloat16)
        part_in = dot(rows, before_grad, 0, 0)
        part_out = dot(value.astype(jnp.bfloat16), grads, 0, 0)
        if s == 0:
            in_ref[...] = part_in
            out_ref[...] = part_out
        else:
            in_ref[...] += part_in
            out_ref[...] += part_out


def expert_weights(everything, w_in, w_out, shards):
    count = everything.shape[0] // (2 * shards)
    return pl.pallas_call(
        functools.partial(expert_weights_kernel, shards, count),
        out_shape=(
            jax.ShapeDtypeStruct(w_in.shape, jnp.float32),
            jax.ShapeDtypeStruct(w_out.shape, jnp.float32),
        ),
        in_specs=in_vmem(3),
        out_specs=tuple(in_vmem(2)),
        compiler_params=pltpu.CompilerParams(vmem_limit_bytes=VMEM_LIMIT),
        cost_estimate=pl.CostEstimate(flops=10**10, bytes_accessed=10**7, transcendentals=10**6),
        name="expert_weights",
    )(everything, w_in, w_out)


def attention_backward_kernel(h, heads, head_size, rows, qkv_ref, bias_ref, grad_ref, out_ref, diag_ref, strip_ref, total_ref):
    length = qkv_ref.shape[1]
    blocks = length // rows
    hd = heads * head_size
    width = bias_ref.shape[1]
    strip_ref[...] = bias_strip(bias_ref[h : h + 1, :], rows)
    total_ref[...] = jnp.zeros_like(total_ref)
    qt32 = qkv_ref[h * head_size : (h + 1) * head_size, :].astype(jnp.float32) * 0.125
    qt = qt32.astype(jnp.bfloat16)
    q = qt32.T.astype(jnp.bfloat16)
    kt = qkv_ref[hd + h * head_size : hd + (h + 1) * head_size, :]
    k = kt.astype(jnp.float32).T.astype(jnp.bfloat16)
    vt = qkv_ref[2 * hd + h * head_size : 2 * hd + (h + 1) * head_size, :]
    gt = grad_ref[h * head_size : (h + 1) * head_size, :]
    g = gt.astype(jnp.float32).T.astype(jnp.bfloat16)
    dk = jnp.zeros((head_size, length), jnp.float32)
    dv = jnp.zeros((head_size, length), jnp.float32)
    for i in range(blocks):
        at = (blocks - 1 - i) * rows
        part = slice(i * rows, (i + 1) * rows)
        s = dot(q[part], kt) + strip_ref[:, at : at + length]
        peak = jnp.max(s, axis=1, keepdims=True)
        p = jnp.exp(s - peak)
        p = p * (1.0 / jnp.sum(p, axis=1, keepdims=True))
        dp = dot(g[part], vt)
        delta = jnp.sum(p * dp, axis=1, keepdims=True)
        ds = p * (dp - delta)
        total_ref[:, at : at + length] += ds
        dsb = ds.astype(jnp.bfloat16)
        dv = dv + dot(gt[:, part], p.astype(jnp.bfloat16))
        dk = dk + dot(qt[:, part], dsb)
        dq = dot(dsb, k) * 0.125
        out_ref[0:head_size, part] = dq.T.astype(jnp.bfloat16)
    out_ref[head_size : 2 * head_size, :] = dk.astype(jnp.bfloat16)
    out_ref[2 * head_size : 3 * head_size, :] = dv.astype(jnp.bfloat16)
    folded = total_ref[...]
    half = rows // 2
    while half:
        folded = folded[:half] + pltpu.roll(folded[half:], width - half, 1)
        half //= 2
    diag_ref[...] = pltpu.roll(folded, rows - 1, 1)


def attention_backward(qkv_t, bias_values, grad_t, h, heads, head_size, rows=256):
    length = qkv_t.shape[1]
    width = bias_values.shape[1]
    return pl.pallas_call(
        functools.partial(attention_backward_kernel, h, heads, head_size, rows),
        out_shape=(jax.ShapeDtypeStruct((3 * head_size, length), jnp.bfloat16), jax.ShapeDtypeStruct((1, width), jnp.float32)),
        in_specs=[pl.BlockSpec(memory_space=pltpu.VMEM)] * 3,
        out_specs=(pl.BlockSpec(memory_space=pltpu.VMEM),) * 2,
        scratch_shapes=[pltpu.VMEM((rows, width), jnp.float32)] * 2,
        compiler_params=pltpu.CompilerParams(vmem_limit_bytes=VMEM_LIMIT),
        cost_estimate=pl.CostEstimate(flops=10 * length * length * head_size * 8, bytes_accessed=4 * qkv_t.size, transcendentals=length * length),
        name="attention_backward",
    )(qkv_t, bias_values, grad_t)


def gelu_pair(v):
    inner = 0.7978845608028654 * (v + 0.044715 * v * v * v)
    t = jnp.tanh(inner)
    slope = 0.7978845608028654 * (1.0 + 3.0 * 0.044715 * v * v)
    return 0.5 * v * (1.0 + t), 0.5 * (1.0 + t) + 0.5 * v * (1.0 - t * t) * slope


def swap(x, axis, k):
    return lax.ppermute(x, axis, [(i, i ^ k) for i in range(lax.axis_size(axis))])


def gather_relative(x, axis="shard"):
    pieces = {0: x}
    bit = lax.axis_size(axis) // 2
    while bit:
        for k in sorted(pieces):
            pieces[k ^ bit] = swap(pieces[k], axis, bit)
        bit //= 2
    return [pieces[k] for k in range(len(pieces))]


def exchange_relative(pieces, axis):
    return [p if k == 0 else swap(p, axis, k) for k, p in enumerate(pieces)]


def sum_all(x, axis):
    if lax.axis_size(axis) > 8:
        return lax.psum(x, axis)
    bit = 1
    while bit < lax.axis_size(axis):
        x = x + swap(x, axis, bit)
        bit *= 2
    return x


def bit_of(me, bit):
    return (me & bit) // bit


def reduce_halves(keep, sent, axis, bits):
    me = lax.axis_index(axis)
    x = keep + swap(sent, axis, bits[0]).astype(jnp.float32)
    for bit in bits[1:]:
        half = x.shape[0] // 2
        high = bit_of(me, bit)
        sent = lax.dynamic_slice_in_dim(x, (1 - high) * half, half, 0).astype(jnp.bfloat16)
        x = lax.dynamic_slice_in_dim(x, high * half, half, 0) + swap(sent, axis, bit).astype(jnp.float32)
    return lax.optimization_barrier(x.astype(jnp.bfloat16))


def gather_halves(x, axis, bits):
    me = lax.axis_index(axis)
    for bit in reversed(bits[1:]):
        high = bit_of(me, bit)
        other = swap(x, axis, bit)
        x = jnp.concatenate([jnp.where(high == 0, x, other), jnp.where(high == 0, other, x)], axis=0)
    return x, swap(x, axis, bits[0])


def on_device(
    inputs,
    cotangent,
    expert_id,
    slot_index,
    bucket_ids,
    attention_gain,
    query_weight,
    key_weight,
    value_weight,
    output_weight,
    bias_table,
    expert_gain,
    router_weight,
    expert_in,
    expert_out,
):
    bf16, f32 = jnp.bfloat16, jnp.float32
    length, width = inputs.shape
    buckets, heads = bias_table.shape
    hd = query_weight.shape[1]
    head_size = hd // heads
    experts = router_weight.shape[1]
    expert_devices = lax.axis_size("expert")
    shards = lax.axis_size("shard")
    me_e = lax.axis_index("expert")
    me_s = lax.axis_index("shard")
    part = max(1, 3 * length // (2 * experts * shards))
    owned = -(-(length + experts * (shards - 1)) // (16 * shards)) * 16
    relative = expert_devices <= 8
    w_in, w_out = expert_in[0], expert_out[0]

    sizes = [part] * expert_devices if relative else [expert_devices * part]

    def exchange_experts(pieces):
        if relative:
            return exchange_relative(pieces, "expert")
        blocks = pieces[0].reshape(expert_devices, part, width)
        return [lax.all_to_all(blocks, "expert", 0, 0).reshape(expert_devices * part, width)]

    ow_pieces = gather_relative(output_weight)
    far_in, far_out = swap(w_in, "shard", 2), swap(w_out, "shard", 2)
    near_in, near_out = swap(w_in, "shard", 1), swap(w_out, "shard", 1)

    residue = slot_index % shards
    group = slot_index // shards
    order = jnp.arange(length, dtype=jnp.int32)
    earlier = (order[None, :] < order[:, None]) & (residue[None, :] == residue[:, None])
    rank = jnp.sum(earlier.astype(jnp.int32), axis=1)
    place = (residue ^ me_s) * owned + rank
    numbers = jnp.arange(shards * owned, dtype=jnp.int32)[:, None]
    perm_flag = numbers == place[None, :]
    perm = perm_flag.astype(bf16)
    perm_absolute = (numbers == (residue * owned + rank)[None, :]).astype(bf16)
    own_flag = perm_flag[:owned]
    own = perm[:owned]

    def packing(expert):
        target = jnp.where(group < part, expert * part + group, -1)
        target_own = jnp.sum(jnp.where(own_flag, target[None, :] + 1, 0), axis=1) - 1
        numbers_own = jnp.arange(experts * part, dtype=jnp.int32)
        return (
            (numbers_own[:, None] == target_own[None, :]).astype(bf16),
            (numbers_own[None, :] == target_own[:, None]).astype(bf16),
        )

    pack, pack_t = packing(expert_id ^ me_e if relative else expert_id)
    expert_own = jnp.sum(jnp.where(own_flag, expert_id[None, :], 0), axis=1)

    offsets = jnp.concatenate([bucket_ids[1:, 0][::-1], bucket_ids[0, :], jnp.full((1,), -1, jnp.int32)])
    bucket_flag = offsets[None, :] == jnp.arange(buckets, dtype=jnp.int32)[:, None]
    bias_values = jnp.sum(jnp.where(bucket_flag[None], bias_table.T[:, :, None], 0.0), axis=1)
    mixed_t, qkv_t, normed = attention_forward(
        inputs, attention_gain[None, :], query_weight, key_weight, value_weight, bias_values, heads, head_size
    )
    mixed_t, cotangent, near_in, near_out, *ow_pieces = lax.optimization_barrier(
        (mixed_t, cotangent, near_in, near_out, *ow_pieces)
    )
    mixed = dot(perm, mixed_t, 1, 1).astype(bf16)
    mixed_own = exchange_relative([mixed[k * owned : (k + 1) * owned] for k in range(shards)], "shard")
    source_own = dot(own, inputs)
    grad_own = dot(own, cotangent).astype(bf16)
    grad_sent = dot(packing(expert_id)[0], grad_own).astype(bf16).reshape(expert_devices, part, width)
    grad_rows = lax.all_to_all(grad_sent, "expert", 0, 0)
    if relative:
        grad_rows = jnp.concatenate([lax.dynamic_index_in_dim(grad_rows, me_e ^ k, 0) for k in range(expert_devices)])
    grad_rows = grad_rows.reshape(expert_devices * part, width)

    middle, routed, probability, *pieces = route_tokens(
        mixed_own, ow_pieces, source_own, pack, expert_gain[None, :], router_weight, sizes
    )
    pieces = exchange_experts(pieces)
    pieces[-1], far_in, far_out = lax.optimization_barrier((pieces[-1], far_in, far_out))
    in_all = (w_in, near_in, far_in, swap(far_in, "shard", 1))
    out_all = (w_out, near_out, far_out, swap(far_out, "shard", 1))

    mine = (jnp.arange(experts, dtype=jnp.int32)[None, :] == me_e).astype(f32)
    slope, both, *outcome = expert_forward(pieces, grad_rows, router_weight, mine, in_all, out_all)
    back_rows = exchange_experts(outcome)
    back_grads = exchange_experts(list(expert_backward(both, slope, in_all, out_all, sizes)))
    both_all = lax.all_gather(both, "shard", axis=0, tiled=True)

    chosen = (expert_own[:, None] == jnp.arange(experts, dtype=jnp.int32)[None, :]).astype(f32)
    token_values, router_part, expert_gain_part, *mixed_grad = token_grads(
        back_rows, back_grads, pack_t, middle, routed, probability, chosen, grad_own, expert_gain[None, :],
        router_weight, ow_pieces,
    )
    mixed_grad = jnp.concatenate(exchange_relative(mixed_grad, "shard"), axis=0)
    mixed_grad_t = dot(mixed_grad, perm, 0, 0).astype(bf16)
    token_values = lax.all_gather(token_values, "shard", axis=0, tiled=True)

    w_heads = jnp.stack([w.reshape(width, heads, head_size) for w in (query_weight, key_weight, value_weight)], axis=2)
    w_heads = w_heads.reshape(width, 3 * hd)
    split = (heads - 1) * 3 * head_size
    w_first, w_last = w_heads[:, :split], w_heads[:, split:]
    head_grads, diagonals = [], []
    for h in range(heads):
        head_grad, diagonal = attention_backward(qkv_t, bias_values, mixed_grad_t, h, heads, head_size)
        head_grads.append(head_grad)
        diagonals.append(diagonal)
    bits = [1 << i for i in range(expert_devices.bit_length() - 1)]
    bits_first, bits_last = bits, [*bits[1:2], *bits[:1], *bits[2:]]
    high_first, high_last = bit_of(me_e, bits_first[0]).reshape(1), bit_of(me_e, bits_last[0]).reshape(1)
    keep_first, sent_first, gain_first = first_parts(normed, head_grads[:-1], w_first, high_first)
    qkv_grad_t = jnp.concatenate(head_grads, axis=0)

    normed_part = dot(qkv_grad_t, w_heads, 0, 1)
    half = length // 2
    low = me_s % 2
    other_half = lax.dynamic_slice_in_dim(normed_part, (1 - low) * half, half, 0)
    own_half = lax.dynamic_slice_in_dim(normed_part, low * half, half, 0)
    normed_grad = own_half + swap(other_half.astype(bf16), "shard", 1).astype(f32)
    bit = 2
    while bit < shards:
        sent = lax.optimization_barrier(normed_grad.astype(bf16))
        normed_grad = sent.astype(f32) + swap(sent, "shard", bit).astype(f32)
        bit *= 2

    middle_grad_all = lax.optimization_barrier(dot(perm_absolute, token_values[:, width:], 0, 0).astype(bf16))
    table_part = jnp.sum(jnp.where(bucket_flag[None], jnp.stack(diagonals), 0.0), axis=2).reshape(-1, 1)
    table_part = jnp.pad(table_part, ((0, width - table_part.shape[0]), (0, 0)))
    small = jnp.concatenate([jnp.zeros_like(table_part), expert_gain_part.T, router_part, table_part], axis=1)
    small = jnp.pad(small, ((0, 0), (0, -small.shape[1] % 128)))
    keep_last, sent_last = last_parts(
        normed, head_grads[-1], w_last, gain_first, attention_gain[:, None], middle_grad_all, mixed_t, small, high_last
    )
    if relative:
        block_first = reduce_halves(keep_first, sent_first, "expert", bits_first)
        block_last = reduce_halves(keep_last, sent_last, "expert", bits_last)
        first = gather_halves(block_first, "expert", bits_first)
        last = gather_halves(block_last, "expert", bits_last)
    else:
        whole = []
        for keep, sent, high in ((keep_first, sent_first, high_first), (keep_last, sent_last, high_last)):
            sent = sent.astype(f32)
            low_part, high_part = jnp.where(high == 0, keep, sent), jnp.where(high == 0, sent, keep)
            low_part, high_part = lax.psum((low_part, high_part), "expert")
            whole.append((jnp.where(high == 0, low_part, high_part), jnp.where(high == 0, high_part, low_part)))
        first, last = whole
    both_all, keep_last = lax.optimization_barrier((both_all, keep_last))
    in_gradient, out_gradient = expert_weights(both_all, w_in, w_out, shards)
    query_gradient, key_gradient, value_gradient, output_gradient, small = place_sums(
        first, last, high_first, high_last, heads, head_size
    )
    table_gradient = small[: buckets * heads, 2 + experts].reshape(heads, buckets).T
    small = sum_all(small[:, : 2 + experts].T, "shard")

    result = dot(perm_absolute, token_values[:, :width], 0, 0).astype(bf16)
    source_half = lax.dynamic_slice_in_dim(inputs, low * half, half, 0).astype(f32)
    inverse_half = lax.rsqrt(jnp.mean(source_half * source_half, axis=-1, keepdims=True) + 1e-06)
    middle_half = lax.dynamic_slice_in_dim(middle_grad_all, low * half, half, 0).astype(f32)
    w = normed_grad * attention_gain
    grad_half = middle_half + inverse_half * w - source_half * (
        inverse_half * inverse_half * inverse_half * jnp.mean(w * source_half, axis=-1, keepdims=True)
    )
    grad_other = swap(grad_half, "shard", 1)
    input_gradient = jnp.concatenate(
        [jnp.where(low == 0, grad_half, grad_other), jnp.where(low == 0, grad_other, grad_half)], axis=0
    )
    return (
        result,
        input_gradient,
        small[0],
        query_gradient,
        key_gradient,
        value_gradient,
        output_gradient,
        table_gradient,
        small[1],
        small[2:].T,
        in_gradient[None],
        out_gradient[None],
    )


def solution(mesh):
    placed = (
        P("expert", None),
        P("expert", None),
        P("expert"),
        P("expert"),
        P(),
        P(),
        P(None, "shard"),
        P(None, "shard"),
        P(None, "shard"),
        P("shard", None),
        P(None, "shard"),
        P(),
        P(),
        P("expert", None, "shard"),
        P("expert", "shard", None),
    )
    return jax.shard_map(
        on_device,
        mesh=mesh,
        in_specs=placed,
        out_specs=(
            P("expert", None),
            P("expert", None),
            P(),
            P(None, "shard"),
            P(None, "shard"),
            P(None, "shard"),
            P("shard", None),
            P(None, "shard"),
            P(),
            P(),
            P("expert", None, "shard"),
            P("expert", "shard", None),
        ),
        check_vma=False,
    )
```

time: 1280 us -> 337 us (0.26)
  local copies, waits for them, and re-layouts: 358 us -> 26.7 us
  blocking collectives: 262 us -> 0 us
  waiting for transfers between devices: 315 us -> 89.5 us
  matrix products: 184 us -> 18.7 us
  Pallas kernels: 0 us -> 98.3 us
  other arithmetic: 108 us -> 14.1 us
  starting transfers between devices: 14.3 us -> 70.3 us
    psum x2 -> x0, blocking collectives: 203 us -> none  [the longest x1 163 us: to_home(): summed = lax.psum(merged, 'shard')]
    psum x3 -> x0, waiting for transfers between devices: 181 us -> none  [the longest x2 114 us: over_heads(): return lax.psum(partial_sums, 'shard')]
    eq x2 -> x0, local copies, waits for them, and re-layouts: 180 us -> none  [scores_at(): bucket_block[:, :, None] == bucket_range[None, None, :]]
    dot_general x41 -> x8, matrix products: 184 us -> 18.7 us  [dot(): lax.dot_general(a, b, (((ca,), (cb,)), ((), ())), preferred_element_type=...]
    all_to_all x3 -> x1, waiting for transfers between devices: 134 us -> 0.01 us  [on_device(): grad_rows = lax.all_to_all(grad_sent, 'expert', 0, 0)]
    pallas_call x0 -> x12, Pallas kernels: none -> 98.3 us  [the longest x4 41.2 us: call(): pl.pallas_call(body, out_shape=out_shape, in_specs=in_vmem(len(args)), ou...]
    dot_general x4 -> x0, local copies, waits for them, and re-layouts: 93.8 us -> none  [scores_at(): jnp.einsum('rkb,bc->crk', indicator, split_table, preferred_element_type=...]
    ppermute x0 -> x53, waiting for transfers between devices: none -> 89.5 us  [swap(): lax.ppermute(x, axis, [(i, i ^ k) for i in range(lax.axis_size(axis))])]
  transfers between devices with their start and end apart: 6 -> 56, of which waited for: 6 -> 25; matrix products, arithmetic and copies ran while one was open for 4% -> 17% of each run, Pallas kernels for 0% -> 20%
where the time goes in v1:
time: 337 us; the launch traced here: 333 us
  Pallas kernels  98.3 us (29%)
  waiting for transfers between devices  89.5 us (27%)
  starting transfers between devices  70.3 us (21%)
  local copies, waits for them, and re-layouts  26.7 us (8%)
  matrix products  18.7 us (6%)
  between operations  15.1 us (4%)
  other arithmetic  14.1 us (4%)
    ppermute x53, waiting for transfers between devices, swap(): lax.ppermute(x, axis, [(i, i ^ k) for i in range(lax.axis_size(axis))])  89.5 us
    ppermute x53, starting transfers between devices, swap(): lax.ppermute(x, axis, [(i, i ^ k) for i in range(lax.axis_size(axis))])  64.1 us
    pallas_call x4, Pallas kernels, call(): pl.pallas_call(body, out_shape=out_shape, in_specs=in_vmem(len(args)), ou...  41.2 us
    pallas_call x3, Pallas kernels, attention_backward(): pl.pallas_call(functools.partial(attention_backward_kernel, h, heads, hea...  20.5 us
    dot_general x8, matrix products, dot(): lax.dot_general(a, b, (((ca,), (cb,)), ((), ())), preferred_element_type=...  18.7 us
    unnamed x137, local copies, waits for them, and re-layouts  16.6 us
    pallas_call x1, Pallas kernels, expert_weights(): pl.pallas_call(functools.partial(expert_weights_kernel, shards, count), o...  14.3 us
    pallas_call x2, Pallas kernels, with_bit(): pl.pallas_call(body, out_shape=out, in_specs=[pl.BlockSpec(memory_space=p...  9.57 us
  transfers between devices with their start and end apart: 56, of which 25 were waited for; matrix products, arithmetic and copies ran while one was open for 17% of the time, Pallas kernels for 20%

profile of v1, /device:TPU:0, one launch (start us, length us, event | category | flops | bytes accessed | tf_op | source)
XLA Modules:
  0.0 332.7 jit_solution(10138224226622790233)
XLA Ops:
  7.8 2.6 collective-permute-start.3
  14.6 1.9 copy.74.wq_ref
  20.4 9.4 %attention_forward.1 = (bf16[192,1024]{1,0:T(8,128)(2,1)}, bf16[576,1024]{1,0:T(8,128)(2,1)}, bf16[1024,768]{1,0:T(8,128)(2,1)}) custom-call(bf16[1024,768]{1,0:T(8,128)(2,1)} %in_ref.1, f32[1,768]{1,0:T(1,128)} %broadcast_in_dim.111.gain_ref, bf16[768,192]{1,0:T(8,128)(2,1)} %copy.74.wq_ref, bf16[768,192]{1,0:T(8,128)(2,1)} %copy.75.wk_ref, ...), custom_call_target="tpu_custom_call" | custom-call | flops 10000000000 | bytes 10000000 | tf_op jit(solution)/shard_map/attention_forward/pallas_call | solution.py:54
  37.0 5.8 %all-to-all-start = ((bf16[8,48,768]{2,1,0:T(8,128)(2,1)}), bf16[8,48,768]{2,1,0:T(8,128)(2,1)S(1)}, u32[]{:S(2)}, u32[]{:S(2)}) async-start(bf16[8,48,768]{2,1,0:T(8,128)(2,1)} %bitcast.4), calls=%async_computation | async-start | bytes 1179648 | tf_op jit(solution)/shard_map/all_to_all | solution.py:541
  48.8 23.1 %collective-permute-done.6.refs_2_ = bf16[272,192]{1,0:T(8,128)(2,1)S(1)} collective-permute-done((bf16[272,192]{1,0:T(8,128)(2,1)S(1)}, bf16[272,192]{1,0:T(8,128)(2,1)S(1)}, u32[]{:S(2)}, u32[]{:S(2)}) %collective-permute-start.6) | collective-permute-done | bytes 104480 | tf_op jit(solution)/shard_map/ppermute | solution.py:407
  72.0 2.4 collective-permute-done.7.refs_3_
  75.1 4.2 %route_tokens.1 = (f32[272,768]{1,0:T(8,128)}, bf16[272,768]{1,0:T(8,128)(2,1)}, f32[272,8]{1,0:T(8,128)}, bf16[48,768]{1,0:T(8,128)(2,1)}, bf16[48,768]{1,0:T(8...) custom-call(bf16[272,192]{1,0:T(8,128)(2,1)} %get-tuple-element.210., ...), custom_call_target="tpu_custom_call" | custom-call | flops 1000000000 | bytes 10000000 | tf_op jit(solution)/shard_map/route_tokens/pallas_call | solution.py:71
  79.3 4.7 %collective-permute-start.14 = (bf16[48,768]{1,0:T(8,128)(2,1)}, bf16[48,768]{1,0:T(8,128)(2,1)S(1)}, u32[]{:S(2)}, u32[]{:S(2)}) collective-permute-start(bf16[48,768]{1,0:T(8,128)(2,1)} %get-tuple-element.94), channel_id=1, source_target_pairs={{0,28},{4,24},{8,20},{12,16},{16,12},{20,8},{24,4},{28,0},{1,29},{... | collective-permute-start | bytes 221192 | tf_op jit(solution)/shard_map/ppermute | solution.py:407
  84.0 3.0 collective-permute-done.14.refs_7_
  94.4 1.9 collective-permute-start.12
  96.9 2.9 collective-permute-start.13
  101.1 3.7 %collective-permute-done.12.refs_5_ = bf16[48,768]{1,0:T(8,128)(2,1)S(1)} collective-permute-done((bf16[48,768]{1,0:T(8,128)(2,1)}, bf16[48,768]{1,0:T(8,128)(2,1)S(1)}, u32[]{:S(2)}, u32[]{:S(2)}) %collective-permute-start.12) | collective-permute-done | bytes 73760 | tf_op jit(solution)/shard_map/ppermute | solution.py:407
  105.4 11.1 %expert_forward.1 = (bf16[384,3072]{1,0:T(8,128)(2,1)}, bf16[768,768]{1,0:T(8,128)(2,1)}, bf16[48,768]{1,0:T(8,128)(2,1)}, bf16[48,768]{1,0:T(8,128)(2,1)}, bf16...) custom-call(bf16[48,768]{1,0:T(8,128)(2,1)} %get-tuple-element.87.re, ...), custom_call_target="tpu_custom_call" | custom-call | flops 4000000000 | bytes 10000000 | tf_op jit(solution)/shard_map/expert_forward/pallas_call | solution.py:71
  120.0 1.9 collective-permute-start.22
  123.3 20.7 %expert_backward.1 = (bf16[48,768]{1,0:T(8,128)(2,1)}, bf16[48,768]{1,0:T(8,128)(2,1)}, bf16[48,768]{1,0:T(8,128)(2,1)}, bf16[48,768]{1,0:T(8,128)(2,1)}, bf16[4...) custom-call(bf16[768,768]{1,0:T(8,128)(2,1)} %get-tuple-element.109.both_ref, ...), custom_call_target="tpu_custom_call" | custom-call | flops 4000000000 | bytes 10000000 | tf_op jit(solution)/shard_map/expert_backward/pallas_call | solution.py:71
  144.1 2.2 collective-permute-start.24
  146.3 2.2 collective-permute-start.25
  150.3 2.5 collective-permute-start.28
  156.2 2.2 collective-permute-start.31
  158.3 2.2 collective-permute-start.32
  161.5 2.3 collective-permute-done.30.refs_13_
  163.8 1.9 collective-permute-done.32.refs_15_
  166.3 5.2 %token_grads.1 = (bf16[272,1536]{1,0:T(8,128)(2,1)}, f32[768,8]{1,0:T(8,128)}, f32[1,768]{1,0:T(1,128)}, bf16[272,192]{1,0:T(8,128)(2,1)}, bf16[272,192]{1,0:T(8...) custom-call(bf16[48,768]{1,0:T(8,128)(2,1)} %get-tuple-element.101.refs_0_, bf16[48,768]{1,0:T(8,128)(2,1)} %copy-done.31, ...), custom_call_target="tpu_custom_call" | custom-call | flops 2000000000 | bytes 10000000 | tf_op jit(solution)/shard_map/token_grads/pallas_call | solution.py:71
  177.9 3.1 collective-permute-done.34
  181.1 2.9 fusion.15.grad_ref
  184.0 6.7 %attention_backward.5 = (bf16[192,1024]{1,0:T(8,128)(2,1)}, f32[1,2048]{1,0:T(1,128)}) custom-call(bf16[576,1024]{1,0:T(8,128)(2,1)} %get-tuple-element.123.qkv_ref, f32[3,2048]{1,0:T(4,128)} %select_reduce_fusion.4.bias_ref, bf16[192,1024]{1,0:T(8,128)(2,1)} %fusion.15.grad_ref), custom_call_target="tpu_custom_call" | custom-call | flops 5368709120 | bytes 2359296 | tf_op jit(solution)/shard_map/attention_backward/pallas_call | solution.py:387
  190.7 6.7 %attention_backward.4 = (bf16[192,1024]{1,0:T(8,128)(2,1)}, f32[1,2048]{1,0:T(1,128)}) custom-call(bf16[576,1024]{1,0:T(8,128)(2,1)} %get-tuple-element.123.qkv_ref, f32[3,2048]{1,0:T(4,128)} %select_reduce_fusion.4.bias_ref, bf16[192,1024]{1,0:T(8,128)(2,1)} %fusion.15.grad_ref), custom_call_target="tpu_custom_call" | custom-call | flops 5368709120 | bytes 2359296 | tf_op jit(solution)/shard_map/attention_backward/pallas_call | solution.py:387
  197.4 7.1 %attention_backward.3 = (bf16[192,1024]{1,0:T(8,128)(2,1)}, f32[1,2048]{1,0:T(1,128)}) custom-call(bf16[576,1024]{1,0:T(8,128)(2,1)} %get-tuple-element.123.qkv_ref, f32[3,2048]{1,0:T(4,128)} %select_reduce_fusion.4.bias_ref, bf16[192,1024]{1,0:T(8,128)(2,1)} %fusion.15.grad_ref), custom_call_target="tpu_custom_call" | custom-call | flops 5368709120 | bytes 2359296 | tf_op jit(solution)/shard_map/attention_backward/pallas_call | solution.py:387
  204.5 4.2 %first_parts.1 = (f32[384,384]{1,0:T(8,128)}, bf16[384,384]{1,0:T(8,128)(2,1)}, f32[768,1]{1,0:T(8,128)}) custom-call(s32[1]{0:T(128)} %bitcast.10.high_ref.first_bit, bf16[1024,768]{1,0:T(8,128)(2,1)} %get-tuple-element.131.normed_ref, bf16[768,384]{1,0:T(8,128)(2,1)} %copy.91.weights_ref, bf16[192,1024]{1,0:T(8,128)(2,1)} %get-tuple-element.128.refs_0_, ...), custom_call_target="tpu_custom_call" | custom-call | flops 2000000000 | bytes 10000000 | tf_op jit(solution)/shard_map/first_parts/pallas_call | solution.py:241
  212.7 5.0 %collective-permute-done.39 = bf16[384,384]{1,0:T(8,128)(2,1)S(1)} collective-permute-done((bf16[384,384]{1,0:T(8,128)(2,1)}, bf16[384,384]{1,0:T(8,128)(2,1)S(1)}, u32[]{:S(2)}, u32[]{:S(2)}) %collective-permute-start.39) | collective-permute-done | bytes 294944 | tf_op jit(solution)/shard_map/ppermute | solution.py:407
  219.3 3.8 %collective-permute-done.40 = bf16[192,384]{1,0:T(8,128)(2,1)S(1)} collective-permute-done((bf16[192,384]{1,0:T(8,128)(2,1)S(1)}, bf16[192,384]{1,0:T(8,128)(2,1)S(1)}, u32[]{:S(2)}, u32[]{:S(2)}) %collective-permute-start.40) | collective-permute-done | bytes 147488 | tf_op jit(solution)/shard_map/ppermute | solution.py:407
  223.1 1.9 collective-permute-start.41
  226.0 3.2 collective-permute-done.41
  230.3 5.0 %fusion.9.middle_ref = bf16[1024,768]{1,0:T(8,128)(2,1)} fusion(s32[1024]{0:T(1024)S(1)} %get-tuple-element.223, bf16[1088,1536]{1,0:T(8,128)(2,1)} %all-gather.3.cloned.1.call-done), kind=kOutput, calls=%fused_computation.18 | convolution fusion | flops 1713176576 | bytes 3248128 | tf_op jit(solution)/shard_map/dot_general | solution.py:13
  235.4 5.4 %last_parts.1 = (f32[384,512]{1,0:T(8,128)}, bf16[384,512]{1,0:T(8,128)(2,1)}) custom-call(s32[1]{0:T(128)} %bitcast.11.high_ref.last_bit, bf16[1024,768]{1,0:T(8,128)(2,1)} %get-tuple-element.131.normed_ref, bf16[192,1024]{1,0:T(8,128)(2,1)} %get-tuple-element.130.head_ref, bf16[768,192]{1,0:T(8,128)(2,1)} %copy.92.weights_ref, ...), custom_call_target="tpu_custom_call" | custom-call | flops 2000000000 | bytes 10000000 | tf_op jit(solution)/shard_map/last_parts/pallas_call | solution.py:241
  245.5 5.4 %collective-permute-done.45 = bf16[384,512]{1,0:T(8,128)(2,1)S(1)} collective-permute-done((bf16[384,512]{1,0:T(8,128)(2,1)}, bf16[384,512]{1,0:T(8,128)(2,1)S(1)}, u32[]{:S(2)}, u32[]{:S(2)}) %collective-permute-start.45) | collective-permute-done | bytes 393248 | tf_op jit(solution)/shard_map/ppermute | solution.py:407
  252.5 5.5 %collective-permute-done.46 = bf16[192,512]{1,0:T(8,128)(2,1)S(1)} collective-permute-done((bf16[192,512]{1,0:T(8,128)(2,1)S(1)}, bf16[192,512]{1,0:T(8,128)(2,1)S(1)}, u32[]{:S(2)}, u32[]{:S(2)}) %collective-permute-start.46) | collective-permute-done | bytes 196640 | tf_op jit(solution)/shard_map/ppermute | solution.py:407
  258.1 1.9 collective-permute-start.47
  260.8 2.2 collective-permute-start.44
  266.4 4.6 %collective-permute-done.48 = bf16[96,512]{1,0:T(8,128)(2,1)S(1)} collective-permute-done((bf16[96,512]{1,0:T(8,128)(2,1)S(1)}, bf16[96,512]{1,0:T(8,128)(2,1)S(1)}, u32[]{:S(2)}, u32[]{:S(2)}) %collective-permute-start.48) | collective-permute-done | bytes 98336 | tf_op jit(solution)/shard_map/ppermute | solution.py:407
  271.5 5.2 %collective-permute-done.49 = bf16[192,512]{1,0:T(8,128)(2,1)S(1)} collective-permute-done((bf16[192,512]{1,0:T(8,128)(2,1)S(1)}, bf16[192,512]{1,0:T(8,128)(2,1)S(1)}, u32[]{:S(2)}, u32[]{:S(2)}) %collective-permute-start.49) | collective-permute-done | bytes 196640 | tf_op jit(solution)/shard_map/ppermute | solution.py:407
  277.8 7.0 %collective-permute-done.50.b1 = bf16[384,512]{1,0:T(8,128)(2,1)} collective-permute-done((bf16[384,512]{1,0:T(8,128)(2,1)S(1)}, bf16[384,512]{1,0:T(8,128)(2,1)}, u32[]{:S(2)}, u32[]{:S(2)}) %collective-permute-start.50) | collective-permute-done | bytes 393248 | tf_op jit(solution)/shard_map/ppermute | solution.py:407
  284.8 3.4 %place_sums.1 = (f32[768,192]{1,0:T(8,128)}, f32[768,192]{1,0:T(8,128)}, f32[768,192]{1,0:T(8,128)}, f32[192,768]{1,0:T(8,128)}, f32[768,128]{1,0:T(8,128)}) custom-call(s32[1]{0:T(128)} %bitcast.10.high_ref.first_bit, s32[1]{0:T(128)} %bitcast.11.high_ref.last_bit, bf16[384,384]{1,0:T(8,128)(2,1)} %pad_maximum_fusion.3.a0, ...), custom_call_target="tpu_custom_call" | custom-call | flops 1000000 | bytes 10000000 | tf_op jit(solution)/shard_map/place_sums/pallas_call | solution.py:298
  289.3 5.1 %fusion.8 = bf16[1024,768]{1,0:T(8,128)(2,1)} fusion(s32[1024]{0:T(1024)S(1)} %get-tuple-element.223, bf16[1088,1536]{1,0:T(8,128)(2,1)} %all-gather.3.cloned.1.call-done), kind=kOutput, calls=%fused_computation.17 | convolution fusion | flops 1713176576 | bytes 3248128 | tf_op jit(solution)/shard_map/dot_general | solution.py:13
  296.2 2.2 copy.86
  298.4 2.2 copy.87
  302.3 3.7 %collective-permute-done.52 = f32[10,768]{0,1:T(8,128)S(1)} collective-permute-done((f32[10,768]{0,1:T(8,128)S(1)}, f32[10,768]{0,1:T(8,128)S(1)}, u32[]{:S(2)}, u32[]{:S(2)}) %collective-permute-start.52) | collective-permute-done | bytes 30752 | tf_op jit(solution)/shard_map/ppermute | solution.py:407
  311.4 14.3 %expert_weights.1 = (f32[768,768]{1,0:T(8,128)}, f32[768,768]{1,0:T(8,128)}) custom-call(bf16[3072,768]{1,0:T(8,128)(2,1)} %all-gather.5.cloned.1.call-done.all_ref, bf16[768,768]{1,0:T(8,128)(2,1)} %bitcast.53, bf16[768,768]{1,0:T(8,128)(2,1)} %bitcast.3.refs_15_.refs_4_.wo_ref), custom_call_target="tpu_custom_call" | custom-call | flops 10000000000 | bytes 10000000 | tf_op jit(solution)/shard_map/expert_weights/pallas_call | solution.py:327
  (288 shorter events, 79.8 us)
Async XLA Ops:
  7.2 26.0 %collective-permute-start.2 = (bf16[192,768]{1,0:T(8,128)(2,1)}, bf16[192,768]{1,0:T(8,128)(2,1)}, u32[]{:S(2)}, u32[]{:S(2)}) collective-permute-start(bf16[192,768]{1,0:T(8,128)(2,1)} %refs_24_), channel_id=1, source_target_pairs={{0,1},{1,0},{2,3},{3,2},{4,5},{5,4},{6,7},{7,6},{8,9},{9,8},{10,11... | collective-permute-start | bytes 884744 | tf_op jit(solution)/shard_map/ppermute | solution.py:407
  7.8 23.5 %collective-permute-start.3 = (bf16[192,768]{1,0:T(8,128)(2,1)}, bf16[192,768]{1,0:T(8,128)(2,1)}, u32[]{:S(2)}, u32[]{:S(2)}) collective-permute-start(bf16[192,768]{1,0:T(8,128)(2,1)} %refs_24_), channel_id=1, source_target_pairs={{0,2},{1,3},{2,0},{3,1},{4,6},{5,7},{6,4},{7,5},{8,10},{9,11},{10,... | collective-permute-start | bytes 884744 | tf_op jit(solution)/shard_map/ppermute | solution.py:407
  10.3 24.7 %collective-permute-start = (bf16[768,768]{1,0:T(8,128)(2,1)}, bf16[768,768]{1,0:T(8,128)(2,1)}, u32[]{:S(2)}, u32[]{:S(2)}) collective-permute-start(bf16[768,768]{1,0:T(8,128)(2,1)} %bitcast.49), channel_id=1, source_target_pairs={{0,1},{1,0},{2,3},{3,2},{4,5},{5,4},{6,7},{7,6},{8,9},{9,8},{10,11... | collective-permute-start | bytes 3538952 | tf_op jit(solution)/shard_map/ppermute | solution.py:407
  10.5 73.5 %collective-permute-start.15 = (bf16[768,768]{1,0:T(8,128)(2,1)}, bf16[768,768]{1,0:T(8,128)(2,1)}, u32[]{:S(2)}, u32[]{:S(2)}) collective-permute-start(bf16[768,768]{1,0:T(8,128)(2,1)} %bitcast.50), channel_id=1, source_target_pairs={{0,2},{1,3},{2,0},{3,1},{4,6},{5,7},{6,4},{7,5},{8,10},{9,11},{10,... | collective-permute-start | bytes 3538952 | tf_op jit(solution)/shard_map/ppermute | solution.py:407
  10.8 24.3 %collective-permute-start.1 = (bf16[768,768]{1,0:T(8,128)(2,1)}, bf16[768,768]{1,0:T(8,128)(2,1)}, u32[]{:S(2)}, u32[]{:S(2)}) collective-permute-start(bf16[768,768]{1,0:T(8,128)(2,1)} %bitcast.3.refs_15_.refs_4_.wo_ref), channel_id=1, source_target_pairs={{0,1},{1,0},{2,3},{3,2},{4,5},{5,4},{6,7},{7,6},{8,9},{9,8},{10,11... | collective-permute-start | bytes 3538952 | tf_op jit(solution)/shard_map/ppermute | solution.py:407
  33.3 50.7 %collective-permute-start.16 = (bf16[768,768]{1,0:T(8,128)(2,1)}, bf16[768,768]{1,0:T(8,128)(2,1)}, u32[]{:S(2)}, u32[]{:S(2)}) collective-permute-start(bf16[768,768]{1,0:T(8,128)(2,1)} %bitcast.3.refs_15_.refs_4_.wo_ref), channel_id=1, source_target_pairs={{0,2},{1,3},{2,0},{3,1},{4,6},{5,7},{6,4},{7,5},{8,10},{9,11},{10,... | collective-permute-start | bytes 3538952 | tf_op jit(solution)/shard_map/ppermute | solution.py:407
  37.0 54.5 %all-to-all-start = ((bf16[8,48,768]{2,1,0:T(8,128)(2,1)}), bf16[8,48,768]{2,1,0:T(8,128)(2,1)S(1)}, u32[]{:S(2)}, u32[]{:S(2)}) async-start(bf16[8,48,768]{2,1,0:T(8,128)(2,1)} %bitcast.4), calls=%async_computation | async-start | bytes 1179648 | tf_op jit(solution)/shard_map/all_to_all | solution.py:541
  42.9 187.5 %all-gather.3.cloned.1.call-start = ((), (), s32[]{:S(2)}) async-start(), calls=%async_computation.1 | async-start | bytes 4177920 | tf_op jit(solution)/shard_map/all_gather | solution.py:567
  44.7 27.2 %collective-permute-start.6 = (bf16[272,192]{1,0:T(8,128)(2,1)S(1)}, bf16[272,192]{1,0:T(8,128)(2,1)S(1)}, u32[]{:S(2)}, u32[]{:S(2)}) collective-permute-start(bf16[272,192]{1,0:T(8,128)(2,1)S(1)} %get-tuple-element.208), channel_id=1, source_target_pairs={{0,2},{1,3},{2,0},{3,1},{4,6},{5,7},{6,4},{7,5},{8,10},{9,11},{10,... | collective-permute-start | bytes 313352 | tf_op jit(solution)/shard_map/ppermute | solution.py:407
  45.3 29.1 %collective-permute-start.7 = (bf16[272,192]{1,0:T(8,128)(2,1)S(1)}, bf16[272,192]{1,0:T(8,128)(2,1)S(1)}, u32[]{:S(2)}, u32[]{:S(2)}) collective-permute-start(bf16[272,192]{1,0:T(8,128)(2,1)S(1)} %get-tuple-element.207), channel_id=1, source_target_pairs={{0,3},{1,2},{2,1},{3,0},{4,7},{5,6},{6,5},{7,4},{8,11},{9,10},{10,... | collective-permute-start | bytes 313352 | tf_op jit(solution)/shard_map/ppermute | solution.py:407
  79.3 7.7 %collective-permute-start.14 = (bf16[48,768]{1,0:T(8,128)(2,1)}, bf16[48,768]{1,0:T(8,128)(2,1)S(1)}, u32[]{:S(2)}, u32[]{:S(2)}) collective-permute-start(bf16[48,768]{1,0:T(8,128)(2,1)} %get-tuple-element.94), channel_id=1, source_target_pairs={{0,28},{4,24},{8,20},{12,16},{16,12},{20,8},{24,4},{28,0},{1,29},{... | collective-permute-start | bytes 221192 | tf_op jit(solution)/shard_map/ppermute | solution.py:407
  87.0 17.8 %collective-permute-start.17 = (bf16[768,768]{1,0:T(8,128)(2,1)}, bf16[768,768]{1,0:T(8,128)(2,1)}, u32[]{:S(2)}, u32[]{:S(2)}) collective-permute-start(bf16[768,768]{1,0:T(8,128)(2,1)} %collective-permute-done.15.refs_13_.refs_2_), channel_id=1, source_target_pairs={{0,1},{1,0},{2,3},{3,2},{4,5},{5,4},{6,7},{7,6},{8,9},{9,8},{10,11... | collective-permute-start | bytes 3538952 | tf_op jit(solution)/shard_map/ppermute | solution.py:407
  87.0 17.8 %collective-permute-start.18 = (bf16[768,768]{1,0:T(8,128)(2,1)}, bf16[768,768]{1,0:T(8,128)(2,1)}, u32[]{:S(2)}, u32[]{:S(2)}) collective-permute-start(bf16[768,768]{1,0:T(8,128)(2,1)} %collective-permute-done.16.refs_17_.refs_6_), channel_id=1, source_target_pairs={{0,1},{1,0},{2,3},{3,2},{4,5},{5,4},{6,7},{7,6},{8,9},{9,8},{10,11... | collective-permute-start | bytes 3538952 | tf_op jit(solution)/shard_map/ppermute | solution.py:407
  90.7 6.3 %collective-permute-start.10 = (bf16[48,768]{1,0:T(8,128)(2,1)}, bf16[48,768]{1,0:T(8,128)(2,1)S(1)}, u32[]{:S(2)}, u32[]{:S(2)}) collective-permute-start(bf16[48,768]{1,0:T(8,128)(2,1)} %get-tuple-element.90), channel_id=1, source_target_pairs={{0,12},{4,8},{8,4},{12,0},{16,28},{20,24},{24,20},{28,16},{1,13},{... | collective-permute-start | bytes 221192 | tf_op jit(solution)/shard_map/ppermute | solution.py:407
  92.6 8.5 %collective-permute-start.11 = (bf16[48,768]{1,0:T(8,128)(2,1)}, bf16[48,768]{1,0:T(8,128)(2,1)S(1)}, u32[]{:S(2)}, u32[]{:S(2)}) collective-permute-start(bf16[48,768]{1,0:T(8,128)(2,1)} %get-tuple-element.91), channel_id=1, source_target_pairs={{0,16},{4,20},{8,24},{12,28},{16,0},{20,4},{24,8},{28,12},{1,17},{... | collective-permute-start | bytes 221192 | tf_op jit(solution)/shard_map/ppermute | solution.py:407
  94.4 10.3 %collective-permute-start.12 = (bf16[48,768]{1,0:T(8,128)(2,1)}, bf16[48,768]{1,0:T(8,128)(2,1)S(1)}, u32[]{:S(2)}, u32[]{:S(2)}) collective-permute-start(bf16[48,768]{1,0:T(8,128)(2,1)} %get-tuple-element.92), channel_id=1, source_target_pairs={{0,20},{4,16},{8,28},{12,24},{16,4},{20,0},{24,12},{28,8},{1,21},{... | collective-permute-start | bytes 221192 | tf_op jit(solution)/shard_map/ppermute | solution.py:407
  96.9 7.8 %collective-permute-start.13 = (bf16[48,768]{1,0:T(8,128)(2,1)}, bf16[48,768]{1,0:T(8,128)(2,1)S(1)}, u32[]{:S(2)}, u32[]{:S(2)}) collective-permute-start(bf16[48,768]{1,0:T(8,128)(2,1)} %get-tuple-element.93), channel_id=1, source_target_pairs={{0,24},{4,28},{8,16},{12,20},{16,8},{20,12},{24,0},{28,4},{1,25},{... | collective-permute-start | bytes 221192 | tf_op jit(solution)/shard_map/ppermute | solution.py:407
  116.5 27.6 %collective-permute-start.19 = (bf16[48,768]{1,0:T(8,128)(2,1)}, bf16[48,768]{1,0:T(8,128)(2,1)S(1)}, u32[]{:S(2)}, u32[]{:S(2)}) collective-permute-start(bf16[48,768]{1,0:T(8,128)(2,1)} %get-tuple-element.102), channel_id=1, source_target_pairs={{0,4},{4,0},{8,12},{12,8},{16,20},{20,16},{24,28},{28,24},{1,5},{5... | collective-permute-start | bytes 221192 | tf_op jit(solution)/shard_map/ppermute | solution.py:407
  117.5 28.8 %collective-permute-start.20 = (bf16[48,768]{1,0:T(8,128)(2,1)}, bf16[48,768]{1,0:T(8,128)(2,1)S(1)}, u32[]{:S(2)}, u32[]{:S(2)}) collective-permute-start(bf16[48,768]{1,0:T(8,128)(2,1)} %get-tuple-element.103), channel_id=1, source_target_pairs={{0,8},{4,12},{8,0},{12,4},{16,24},{20,28},{24,16},{28,20},{1,9},{5... | collective-permute-start | bytes 221192 | tf_op jit(solution)/shard_map/ppermute | solution.py:407
  118.4 30.2 %collective-permute-start.21 = (bf16[48,768]{1,0:T(8,128)(2,1)}, bf16[48,768]{1,0:T(8,128)(2,1)S(1)}, u32[]{:S(2)}, u32[]{:S(2)}) collective-permute-start(bf16[48,768]{1,0:T(8,128)(2,1)} %get-tuple-element.104), channel_id=1, source_target_pairs={{0,12},{4,8},{8,4},{12,0},{16,28},{20,24},{24,20},{28,16},{1,13},{... | collective-permute-start | bytes 221192 | tf_op jit(solution)/shard_map/ppermute | solution.py:407
  120.0 29.5 %collective-permute-start.22 = (bf16[48,768]{1,0:T(8,128)(2,1)}, bf16[48,768]{1,0:T(8,128)(2,1)S(1)}, u32[]{:S(2)}, u32[]{:S(2)}) collective-permute-start(bf16[48,768]{1,0:T(8,128)(2,1)} %get-tuple-element.105), channel_id=1, source_target_pairs={{0,16},{4,20},{8,24},{12,28},{16,0},{20,4},{24,8},{28,12},{1,17},{... | collective-permute-start | bytes 221192 | tf_op jit(solution)/shard_map/ppermute | solution.py:407
  122.0 28.4 %collective-permute-start.23 = (bf16[48,768]{1,0:T(8,128)(2,1)}, bf16[48,768]{1,0:T(8,128)(2,1)S(1)}, u32[]{:S(2)}, u32[]{:S(2)}) collective-permute-start(bf16[48,768]{1,0:T(8,128)(2,1)} %get-tuple-element.106), channel_id=1, source_target_pairs={{0,20},{4,16},{8,28},{12,24},{16,4},{20,0},{24,12},{28,8},{1,21},{... | collective-permute-start | bytes 221192 | tf_op jit(solution)/shard_map/ppermute | solution.py:407
  144.1 8.8 %collective-permute-start.24 = (bf16[48,768]{1,0:T(8,128)(2,1)S(1)}, bf16[48,768]{1,0:T(8,128)(2,1)S(1)}, u32[]{:S(2)}, u32[]{:S(2)}) collective-permute-start(bf16[48,768]{1,0:T(8,128)(2,1)S(1)} %copy-done.41), channel_id=1, source_target_pairs={{0,24},{4,28},{8,16},{12,20},{16,8},{20,12},{24,0},{28,4},{1,25},{... | collective-permute-start | bytes 221192 | tf_op jit(solution)/shard_map/ppermute | solution.py:407
  146.3 8.0 %collective-permute-start.25 = (bf16[48,768]{1,0:T(8,128)(2,1)S(1)}, bf16[48,768]{1,0:T(8,128)(2,1)S(1)}, u32[]{:S(2)}, u32[]{:S(2)}) collective-permute-start(bf16[48,768]{1,0:T(8,128)(2,1)S(1)} %copy-done.39), channel_id=1, source_target_pairs={{0,28},{4,24},{8,20},{12,16},{16,12},{20,8},{24,4},{28,0},{1,29},{... | collective-permute-start | bytes 221192 | tf_op jit(solution)/shard_map/ppermute | solution.py:407
  148.6 7.6 %collective-permute-start.26 = (bf16[48,768]{1,0:T(8,128)(2,1)}, bf16[48,768]{1,0:T(8,128)(2,1)S(1)}, u32[]{:S(2)}, u32[]{:S(2)}) collective-permute-start(bf16[48,768]{1,0:T(8,128)(2,1)} %get-tuple-element.112), channel_id=1, source_target_pairs={{0,4},{4,0},{8,12},{12,8},{16,20},{20,16},{24,28},{28,24},{1,5},{5... | collective-permute-start | bytes 221192 | tf_op jit(solution)/shard_map/ppermute | solution.py:407
  149.5 8.8 %collective-permute-start.27 = (bf16[48,768]{1,0:T(8,128)(2,1)}, bf16[48,768]{1,0:T(8,128)(2,1)S(1)}, u32[]{:S(2)}, u32[]{:S(2)}) collective-permute-start(bf16[48,768]{1,0:T(8,128)(2,1)} %get-tuple-element.113), channel_id=1, source_target_pairs={{0,8},{4,12},{8,0},{12,4},{16,24},{20,28},{24,16},{28,20},{1,9},{5... | collective-permute-start | bytes 221192 | tf_op jit(solution)/shard_map/ppermute | solution.py:407
  150.3 11.0 %collective-permute-start.28 = (bf16[48,768]{1,0:T(8,128)(2,1)}, bf16[48,768]{1,0:T(8,128)(2,1)S(1)}, u32[]{:S(2)}, u32[]{:S(2)}) collective-permute-start(bf16[48,768]{1,0:T(8,128)(2,1)} %get-tuple-element.114), channel_id=1, source_target_pairs={{0,12},{4,8},{8,4},{12,0},{16,28},{20,24},{24,20},{28,16},{1,13},{... | collective-permute-start | bytes 221192 | tf_op jit(solution)/shard_map/ppermute | solution.py:407
  152.9 8.7 %collective-permute-start.29 = (bf16[48,768]{1,0:T(8,128)(2,1)}, bf16[48,768]{1,0:T(8,128)(2,1)S(1)}, u32[]{:S(2)}, u32[]{:S(2)}) collective-permute-start(bf16[48,768]{1,0:T(8,128)(2,1)} %get-tuple-element.115), channel_id=1, source_target_pairs={{0,16},{4,20},{8,24},{12,28},{16,0},{20,4},{24,8},{28,12},{1,17},{... | collective-permute-start | bytes 221192 | tf_op jit(solution)/shard_map/ppermute | solution.py:407
  154.3 9.5 %collective-permute-start.30 = (bf16[48,768]{1,0:T(8,128)(2,1)}, bf16[48,768]{1,0:T(8,128)(2,1)S(1)}, u32[]{:S(2)}, u32[]{:S(2)}) collective-permute-start(bf16[48,768]{1,0:T(8,128)(2,1)} %get-tuple-element.116), channel_id=1, source_target_pairs={{0,20},{4,16},{8,28},{12,24},{16,4},{20,0},{24,12},{28,8},{1,21},{... | collective-permute-start | bytes 221192 | tf_op jit(solution)/shard_map/ppermute | solution.py:407
  156.2 7.6 %collective-permute-start.31 = (bf16[48,768]{1,0:T(8,128)(2,1)}, bf16[48,768]{1,0:T(8,128)(2,1)S(1)}, u32[]{:S(2)}, u32[]{:S(2)}) collective-permute-start(bf16[48,768]{1,0:T(8,128)(2,1)} %get-tuple-element.117), channel_id=1, source_target_pairs={{0,24},{4,28},{8,16},{12,20},{16,8},{20,12},{24,0},{28,4},{1,25},{... | collective-permute-start | bytes 221192 | tf_op jit(solution)/shard_map/ppermute | solution.py:407
  158.3 7.4 %collective-permute-start.32 = (bf16[48,768]{1,0:T(8,128)(2,1)}, bf16[48,768]{1,0:T(8,128)(2,1)S(1)}, u32[]{:S(2)}, u32[]{:S(2)}) collective-permute-start(bf16[48,768]{1,0:T(8,128)(2,1)} %get-tuple-element.118), channel_id=1, source_target_pairs={{0,28},{4,24},{8,20},{12,16},{16,12},{20,8},{24,4},{28,0},{1,29},{... | collective-permute-start | bytes 221192 | tf_op jit(solution)/shard_map/ppermute | solution.py:407
  171.6 139.9 %all-gather.5.cloned.1.call-start = ((), (), s32[]{:S(2)}) async-start(), calls=%async_computation.2 | async-start | bytes 5898240 | tf_op jit(solution)/shard_map/all_gather | solution.py:558
  171.7 6.2 %collective-permute-start.35 = (bf16[272,192]{1,0:T(8,128)(2,1)}, bf16[272,192]{1,0:T(8,128)(2,1)}, u32[]{:S(2)}, u32[]{:S(2)}) collective-permute-start(bf16[272,192]{1,0:T(8,128)(2,1)} %get-tuple-element.127), channel_id=1, source_target_pairs={{0,3},{1,2},{2,1},{3,0},{4,7},{5,6},{6,5},{7,4},{8,11},{9,10},{10,... | collective-permute-start | bytes 313352 | tf_op jit(solution)/shard_map/ppermute | solution.py:407
  171.8 9.3 %collective-permute-start.34 = (bf16[272,192]{1,0:T(8,128)(2,1)}, bf16[272,192]{1,0:T(8,128)(2,1)}, u32[]{:S(2)}, u32[]{:S(2)}) collective-permute-start(bf16[272,192]{1,0:T(8,128)(2,1)} %get-tuple-element.126), channel_id=1, source_target_pairs={{0,2},{1,3},{2,0},{3,1},{4,6},{5,7},{6,4},{7,5},{8,10},{9,11},{10,... | collective-permute-start | bytes 313352 | tf_op jit(solution)/shard_map/ppermute | solution.py:407
  173.4 7.7 %collective-permute-start.33 = (bf16[272,192]{1,0:T(8,128)(2,1)}, bf16[272,192]{1,0:T(8,128)(2,1)}, u32[]{:S(2)}, u32[]{:S(2)}) collective-permute-start(bf16[272,192]{1,0:T(8,128)(2,1)} %get-tuple-element.125), channel_id=1, source_target_pairs={{0,1},{1,0},{2,3},{3,2},{4,5},{5,4},{6,7},{7,6},{8,9},{9,8},{10,11... | collective-permute-start | bytes 313352 | tf_op jit(solution)/shard_map/ppermute | solution.py:407
  208.7 9.1 %collective-permute-start.39 = (bf16[384,384]{1,0:T(8,128)(2,1)}, bf16[384,384]{1,0:T(8,128)(2,1)S(1)}, u32[]{:S(2)}, u32[]{:S(2)}) collective-permute-start(bf16[384,384]{1,0:T(8,128)(2,1)} %get-tuple-element.133), channel_id=1, source_target_pairs={{0,4},{4,0},{8,12},{12,8},{16,20},{20,16},{24,28},{28,24},{1,5},{5... | collective-permute-start | bytes 884744 | tf_op jit(solution)/shard_map/ppermute | solution.py:407
  212.7 30.3 %collective-permute-start.36 = (bf16[512,768]{1,0:T(8,128)(2,1)}, bf16[512,768]{1,0:T(8,128)(2,1)}, u32[]{:S(2)}, u32[]{:S(2)}) collective-permute-start(bf16[512,768]{1,0:T(8,128)(2,1)} %dynamic-slice_convert_fusion), channel_id=1, source_target_pairs={{0,1},{1,0},{2,3},{3,2},{4,5},{5,4},{6,7},{7,6},{8,9},{9,8},{10,11... | collective-permute-start | bytes 2359304 | tf_op jit(solution)/shard_map/ppermute | solution.py:407
  229.2 12.2 %collective-permute-start.42 = (bf16[96,384]{1,0:T(8,128)(2,1)S(1)}, bf16[96,384]{1,0:T(8,128)(2,1)S(1)}, u32[]{:S(2)}, u32[]{:S(2)}) collective-permute-start(bf16[96,384]{1,0:T(8,128)(2,1)S(1)} %add_convert_fusion.2), channel_id=1, source_target_pairs={{0,16},{4,20},{8,24},{12,28},{16,0},{20,4},{24,8},{28,12},{1,17},{... | collective-permute-start | bytes 221192 | tf_op jit(solution)/shard_map/ppermute | solution.py:407
  240.8 10.1 %collective-permute-start.45 = (bf16[384,512]{1,0:T(8,128)(2,1)}, bf16[384,512]{1,0:T(8,128)(2,1)S(1)}, u32[]{:S(2)}, u32[]{:S(2)}) collective-permute-start(bf16[384,512]{1,0:T(8,128)(2,1)} %get-tuple-element.141), channel_id=1, source_target_pairs={{0,8},{4,12},{8,0},{12,4},{16,24},{20,28},{24,16},{28,20},{1,9},{5... | collective-permute-start | bytes 1179656 | tf_op jit(solution)/shard_map/ppermute | solution.py:407
  241.5 11.0 %collective-permute-start.43 = (bf16[192,384]{1,0:T(8,128)(2,1)S(1)}, bf16[192,384]{1,0:T(8,128)(2,1)S(1)}, u32[]{:S(2)}, u32[]{:S(2)}) collective-permute-start(bf16[192,384]{1,0:T(8,128)(2,1)S(1)} %pad_maximum_fusion.5), channel_id=1, source_target_pairs={{0,8},{4,12},{8,0},{12,4},{16,24},{20,28},{24,16},{28,20},{1,9},{5... | collective-permute-start | bytes 442376 | tf_op jit(solution)/shard_map/ppermute | solution.py:407
  244.3 21.5 %collective-permute-start.37 = (bf16[512,768]{1,0:T(8,128)(2,1)S(1)}, bf16[512,768]{1,0:T(8,128)(2,1)S(1)}, u32[]{:S(2)}, u32[]{:S(2)}) collective-permute-start(bf16[512,768]{1,0:T(8,128)(2,1)S(1)} %add_convert_fusion), channel_id=1, source_target_pairs={{0,2},{1,3},{2,0},{3,1},{4,6},{5,7},{6,4},{7,5},{8,10},{9,11},{10,... | collective-permute-start | bytes 2359304 | tf_op jit(solution)/shard_map/ppermute | solution.py:407
  251.0 7.0 %collective-permute-start.46 = (bf16[192,512]{1,0:T(8,128)(2,1)S(1)}, bf16[192,512]{1,0:T(8,128)(2,1)S(1)}, u32[]{:S(2)}, u32[]{:S(2)}) collective-permute-start(bf16[192,512]{1,0:T(8,128)(2,1)S(1)} %dynamic-slice_convert_fusion.1), channel_id=1, source_target_pairs={{0,4},{4,0},{8,12},{12,8},{16,20},{20,16},{24,28},{28,24},{1,5},{5... | collective-permute-start | bytes 589832 | tf_op jit(solution)/shard_map/ppermute | solution.py:407
  258.1 6.6 %collective-permute-start.47 = (bf16[96,512]{1,0:T(8,128)(2,1)S(1)}, bf16[96,512]{1,0:T(8,128)(2,1)S(1)}, u32[]{:S(2)}, u32[]{:S(2)}) collective-permute-start(bf16[96,512]{1,0:T(8,128)(2,1)S(1)} %dynamic-slice_convert_fusion.3), channel_id=1, source_target_pairs={{0,16},{4,20},{8,24},{12,28},{16,0},{20,4},{24,8},{28,12},{1,17},{... | collective-permute-start | bytes 294920 | tf_op jit(solution)/shard_map/ppermute | solution.py:407
  260.8 17.0 %collective-permute-start.44 = (bf16[384,384]{1,0:T(8,128)(2,1)}, bf16[384,384]{1,0:T(8,128)(2,1)}, u32[]{:S(2)}, u32[]{:S(2)}) collective-permute-start(bf16[384,384]{1,0:T(8,128)(2,1)} %pad_maximum_fusion.3.a0), channel_id=1, source_target_pairs={{0,4},{4,0},{8,12},{12,8},{16,20},{20,16},{24,28},{28,24},{1,5},{5... | collective-permute-start | bytes 884744 | tf_op jit(solution)/shard_map/ppermute | solution.py:407
  264.8 6.2 %collective-permute-start.48 = (bf16[96,512]{1,0:T(8,128)(2,1)S(1)}, bf16[96,512]{1,0:T(8,128)(2,1)S(1)}, u32[]{:S(2)}, u32[]{:S(2)}) collective-permute-start(bf16[96,512]{1,0:T(8,128)(2,1)S(1)} %add_convert_fusion.1), channel_id=1, source_target_pairs={{0,16},{4,20},{8,24},{12,28},{16,0},{20,4},{24,8},{28,12},{1,17},{... | collective-permute-start | bytes 294920 | tf_op jit(solution)/shard_map/ppermute | solution.py:407
  276.9 7.9 %collective-permute-start.50 = (bf16[384,512]{1,0:T(8,128)(2,1)S(1)}, bf16[384,512]{1,0:T(8,128)(2,1)}, u32[]{:S(2)}, u32[]{:S(2)}) collective-permute-start(bf16[384,512]{1,0:T(8,128)(2,1)S(1)} %pad_maximum_fusion.2.b0), channel_id=1, source_target_pairs={{0,8},{4,12},{8,0},{12,4},{16,24},{20,28},{24,16},{28,20},{1,9},{5... | collective-permute-start | bytes 1179656 | tf_op jit(solution)/shard_map/ppermute | solution.py:407
  277.7 30.3 %collective-permute-start.38 = (f32[512,768]{1,0:T(8,128)S(1)}, f32[512,768]{1,0:T(8,128)}, u32[]{:S(2)}, u32[]{:S(2)}) collective-permute-start(f32[512,768]{1,0:T(8,128)S(1)} %fusion.14), channel_id=1, source_target_pairs={{0,1},{1,0},{2,3},{3,2},{4,5},{5,4},{6,7},{7,6},{8,9},{9,8},{10,11... | collective-permute-start | bytes 4718600 | tf_op jit(solution)/shard_map/ppermute | solution.py:407
  294.4 11.5 %collective-permute-start.52 = (f32[10,768]{0,1:T(8,128)S(1)}, f32[10,768]{0,1:T(8,128)S(1)}, u32[]{:S(2)}, u32[]{:S(2)}) collective-permute-start(f32[10,768]{0,1:T(8,128)S(1)} %fusion.41), channel_id=1, source_target_pairs={{0,2},{1,3},{2,0},{3,1},{4,6},{5,7},{6,4},{7,5},{8,10},{9,11},{10,... | collective-permute-start | bytes 92168 | tf_op jit(solution)/shard_map/ppermute | solution.py:407
  (68 other events, 573.9 us)
Sparse Core Ops, SparseCore 0:
  171.7 28.6 all-gather.2
  202.0 37.3 all-gather.4
